TPU v7x, 128 devices: a whole 4x4x4 slice. The times are simulated.
128 devices in a mesh: occ: 8 (over z_lo, y), vir: 16 (over x, z_hi, core).
Axes of the slice: x: 4, y: 4, z: 4 (z_hi: 2, z_lo: 2; z = z_hi * 2 + z_lo), core: 2. Of those that a mesh axis runs over, the one named last changes fastest.
Arguments:
- lam: bfloat16 [8192, 28672], P('occ', 'vir'), may hold values from -6 to 6
- ladder_int: bfloat16 [28672, 4096], P('vir'), may hold values from -0.046875 to 0.046875
- cycle_amp: bfloat16 [1024, 3200], P('occ'), may hold values from -6 to 6
- cycle_int: bfloat16 [3200, 32768], P('occ', 'vir'), may hold values from -0.3125 to 0.3125
- occ_irrep: int32 [200], replicated, may hold values from 0 to 7, as said below
- virt_irrep: int32 [256], replicated, may hold values from 0 to 7, as said below
Outputs:
- residual: float32 [1024, 32768], P('occ', 'vir')
Inputs may be any that keep to these rules, and one draw needn't show every extreme that they name: `occ_irrep`: nondecreasing along the orbitals (contiguous symmetry blocks); every label 0 to 7 occurs. `virt_irrep`: nondecreasing along the orbitals (contiguous symmetry blocks); every label 0 to 7 occurs.
All inputs are finite; a program needn't handle non-finite values.
Results may differ from a plain program's by a relative error of at most 0.0003.
Values may be sent and summed in bfloat16 or wider, within the bound.
No kernel may reach another device: no remote copies, remote signals or barrier semaphores. Data moves between devices by JAX's collectives and lax.ppermute only.
A program may use at most 128 MiB of HBM per device.

v0:
```python
import jax
import jax.numpy as jnp
from jax import lax
from jax.sharding import PartitionSpec as P

PAN = 16
AW = 16
BW = 256
JW = 128


def per_device(lam, ladder_int, cycle_amp, cycle_int, occ_irrep, virt_irrep):
    vir_count = lax.axis_size("vir")
    row_count = lam.shape[0]
    i_dev = row_count // JW
    j_width = JW // vir_count
    lam_blocks = lam.reshape(i_dev, JW, lam.shape[1])
    ladder_part = lax.psum_scatter(
        jnp.einsum("ijk,kn->jin", lam_blocks, ladder_int, preferred_element_type=jnp.float32),
        "vir",
        scatter_dimension=0,
        tiled=True,
    )
    regrouped = (
        ladder_part.reshape(j_width, i_dev, AW, BW)
        .transpose(1, 2, 0, 3)
        .reshape(i_dev * AW, j_width * BW)
    )
    j_first = lax.axis_index("vir") * j_width
    j_irrep = lax.dynamic_slice_in_dim(occ_irrep, j_first, j_width, 0)
    jb_irrep = (j_irrep[:, None] ^ virt_irrep[None, :]).reshape(-1)
    kc_irrep = (occ_irrep[:, None] ^ virt_irrep[None, :PAN]).reshape(-1)
    zero_value = jnp.zeros((), cycle_int.dtype)
    masked = jnp.where(
        kc_irrep[:, None] == jb_irrep[None, :],
        lax.all_gather(cycle_int, "occ", axis=0, tiled=True),
        zero_value,
    )
    cycle = jnp.dot(cycle_amp, masked, preferred_element_type=jnp.float32)
    return regrouped + cycle


def solution(mesh):
    return jax.shard_map(
        per_device,
        mesh=mesh,
        in_specs=(P("occ", "vir"), P("vir", None), P("occ", None), P("occ", "vir"), P(), P()),
        out_specs=P("occ", "vir"),
        check_vma=False,
    )
```

profile of v0, /device:TPU:0, one launch (start us, length us, event | category | flops | bytes accessed | tf_op | source)
XLA Modules:
  0.0 311.1 jit_solution(3719788325727757453)
XLA Ops:
  7.4 0.0 copy-start
  7.4 0.0 reduce-scatter.2.cloned.1.call-start
  7.4 21.2 %fusion.5 = f32[128,8,4096]{0,2,1:T(8,128)} fusion(bf16[8,128,1792]{2,1,0:T(8,128)(2,1)} %bitcast.26, bf16[1792,4096]{1,0:T(8,128)(2,1)} %param.7), kind=kOutput, calls=%fused_computation.6 | convolution fusion | flops 15032385536 | bytes 35127296 | tf_op jit(solution)/shard_map/ijk,kn->jin/dot_general | solution.py:19
  28.6 17.7 %copy.15 = f32[128,8,4096]{2,1,0:T(8,128)} copy(f32[128,8,4096]{0,2,1:T(8,128)} %fusion.5) | data formatting | bytes 33554432 | tf_op jit(solution)/shard_map/ijk,kn->jin/transpose | solution.py:19
  46.4 0.0 copy-start.1
  46.4 0.0 copy-start.2
  46.4 0.0 slice-start
  46.4 0.0 reduce-scatter.2.cloned.1.call-update
  46.4 0.0 all-gather.2.cloned.1.call-start
  46.4 0.5 all-gather.2.cloned.1.call-update
  47.0 0.1 copy-done.1
  47.0 0.1 dynamic_slice.3
  47.1 0.0 copy-done.2
  47.1 0.1 xor_bitcast_fusion
  47.2 0.0 slice-done
  47.2 0.1 broadcast_xor_fusion
  47.3 0.1 xor.43
  47.4 243.2 %reduce-scatter.2.cloned.1.call-done = f32[8,8,4096]{2,1,0:T(8,128)} async-done(((f32[128,8,4096]{2,1,0:T(8,128)}), f32[8,8,4096]{2,1,0:T(8,128)}) %reduce-scatter.2.cloned.1.call-update) | async-done | bytes 1048592 | tf_op jit(solution)/shard_map/reduce_scatter | solution.py:18
  290.6 1.8 copy.16
  292.5 0.3 copy.21
  292.8 0.3 copy.17
  293.1 0.0 all-gather.2.cloned.1.call-done
  293.2 0.0 copy-done
  293.2 9.1 %fusion.10 = f32[128,2048]{0,1:T(8,128)S(1)} fusion(f32[128,2048]{0,1:T(8,128)S(1)} %copy.17, bf16[128,3200]{1,0:T(8,128)(2,1)S(1)} %copy-done, bf16[3200,2048]{1,0:T(8,128)(2,1)} %all-gather.2.cloned.1.call-done, s32[2048]{0:T(1024)S(1)} %bitcast.25, s32[3200]{0:T(1024)S(1)} %xor.43), kind=kOutput, calls=%fused_computation.9 | convolution fusion | flops 1691090944 | bytes 16044544 | tf_op jit(solution)/shard_map/dot_general | solution.py:39
  302.3 1.3 copy.18
  (1 shorter events, 0.0 us)
Async XLA Ops:
  7.4 285.8 %copy-start = (bf16[128,3200]{1,0:T(8,128)(2,1)S(1)}, bf16[128,3200]{1,0:T(8,128)(2,1)}, u32[]{:S(2)}) copy-start(bf16[128,3200]{1,0:T(8,128)(2,1)} %param.8) | copy-start | bytes 2457604
  7.4 283.2 %reduce-scatter.2.cloned.1.call-start = ((), (), s32[]{:S(2)}) async-start(), calls=%async_computation.1 | async-start | bytes 17825792 | tf_op jit(solution)/shard_map/reduce_scatter | solution.py:18
  46.4 0.7 copy-start.1
  46.4 0.8 copy-start.2
  46.4 0.8 slice-start
  46.4 246.8 %all-gather.2.cloned.1.call-start = ((), (), s32[]{:S(2)}) async-start(), calls=%async_computation.2 | async-start | bytes 14745600 | tf_op jit(solution)/shard_map/all_gather | solution.py:36
Sparse Core Ops, SparseCore 0:
  46.5 244.0 reduce-scatter.1
Sparse Core Ops, SparseCore 1:
  48.6 138.7 all-gather.1
where the time goes:
time: 312 us; the launch traced here: 311 us
  waiting for transfers between devices  244 us (78%)
  matrix products  30.4 us (10%)
  local copies, waits for them, and re-layouts  21.8 us (7%)
  between operations  14.9 us (5%)
    reduce_scatter x1, waiting for transfers between devices, per_device(): lax.psum_scatter(jnp.einsum('ijk,kn->jin', lam_blocks, ladder_int, prefer...  243 us
    dot_general x1, matrix products, per_device(): jnp.einsum('ijk,kn->jin', lam_blocks, ladder_int, preferred_element_type=...  21.2 us
    transpose x1, local copies, waits for them, and re-layouts, per_device(): jnp.einsum('ijk,kn->jin', lam_blocks, ladder_int, preferred_element_type=...  17.7 us
    dot_general x1, matrix products, per_device(): cycle = jnp.dot(cycle_amp, masked, preferred_element_type=jnp.float32)  9.13 us
  transfers between devices with their start and end apart: 2, of which 1 were waited for; matrix products, arithmetic and copies ran while one was open for 1% of the time, Pallas kernels for 0%

commit v1 on v0

v1 whole, which is shorter than its diff:
```python
import functools

import jax
import jax.numpy as jnp
from jax import lax
from jax.experimental import pallas as pl
from jax.experimental.pallas import tpu as pltpu
from jax.sharding import Mesh, PartitionSpec as P

PAN = 16
AW = 16
BW = 256
JW = 128
LANES = 128
SCALE_ROWS = 16
SEGMENT = 64
Z_COLUMNS = 2048
TILE = 512
VMEM_BYTES = 56 * 1024 * 1024

VIR = ("x", "z_hi", "core")
OCC = ("z_lo", "y")


def encode(block):
    top = jnp.maximum(jnp.max(jnp.abs(block), axis=0, keepdims=True), 1e-30)
    level = jnp.ceil(jnp.log2(top) * 256.0) + 1.0
    step = jnp.exp2(level * (-1.0 / 256.0)) * 32767.0
    return jnp.round(block * step).astype(jnp.int32).astype(jnp.int16), level


def decode(code, level):
    step = jnp.exp2(level * (1.0 / 256.0)) * (1.0 / 32767.0)
    return code.astype(jnp.int32).astype(jnp.float32) * step


def level_rows(levels):
    spare = jnp.zeros((1, LANES), jnp.float32)
    rows = jnp.concatenate(levels + [spare] * (SCALE_ROWS - len(levels)), axis=0)
    return rows.astype(jnp.int32).astype(jnp.int16)


def read_levels(block):
    return block.astype(jnp.int32).astype(jnp.float32)


def params(**more):
    return pltpu.CompilerParams(vmem_limit_bytes=VMEM_BYTES, **more)


def cost(rows, depth, columns, more=0):
    return pl.CostEstimate(
        flops=2 * rows * depth * columns,
        bytes_accessed=2 * (rows * depth + depth * columns) + more,
        transcendentals=0,
    )


def columns_of(block):
    return pl.ds(block * LANES, LANES)


def partner_kernel(lam_ref, panel_ref, out_ref):
    rows = lam_ref.shape[0]
    acc = jnp.dot(lam_ref[...], panel_ref[...], preferred_element_type=jnp.float32)
    blocks = acc.shape[1] // LANES
    levels = []
    for block in range(blocks):
        code, level = encode(acc[:, block * LANES : (block + 1) * LANES])
        out_ref[0, block * rows : (block + 1) * rows, :] = code
        levels.append(level)
    out_ref[0, blocks * rows :, :] = level_rows(levels)


def partner_part(lam_rows, panel, first, width):
    rows, depth = lam_rows.shape
    tiles, offset = width // TILE, first // TILE
    size = TILE // LANES * rows + SCALE_ROWS
    return pl.pallas_call(
        partner_kernel,
        grid=(tiles,),
        in_specs=[
            pl.BlockSpec((rows, depth), lambda t: (0, 0)),
            pl.BlockSpec((depth, TILE), lambda t: (0, t + offset)),
        ],
        out_specs=pl.BlockSpec((1, size, LANES), lambda t: (t, 0, 0)),
        out_shape=jax.ShapeDtypeStruct((tiles, size, LANES), jnp.int16),
        compiler_params=params(),
        cost_estimate=cost(rows, depth, width),
        name="partner_part",
    )(lam_rows, panel)


def own_sum(lam_ref, panel_ref, recv_ref):
    rows = lam_ref.shape[0]
    acc = jnp.dot(lam_ref[...], panel_ref[...], preferred_element_type=jnp.float32)
    blocks = acc.shape[1] // LANES
    levels = read_levels(recv_ref[0, blocks * rows :, :])
    sums = []
    for block in range(blocks):
        got = decode(recv_ref[0, block * rows : (block + 1) * rows, :], levels[block : block + 1, :])
        sums.append(acc[:, block * LANES : (block + 1) * LANES] + got)
    return sums


def target_rows(total, x_dev, z_dev, i_dev):
    pieces = [total[(i * 8 + x_dev * 2 + z_dev) * 8 : (i * 8 + x_dev * 2 + z_dev) * 8 + 8, :] for i in range(i_dev)]
    return jnp.concatenate(pieces, axis=0)


def own_z_kernel(z_ref, lam_ref, panel_ref, recv_ref, send_ref, keep_ref):
    i_dev = lam_ref.shape[0] // 64
    here = z_ref[0]
    sums = own_sum(lam_ref, panel_ref, recv_ref)
    levels = []
    size = 4 * i_dev * 8
    for block, total in enumerate(sums):
        low = jnp.concatenate([target_rows(total, x, 0, i_dev) for x in range(4)], axis=0)
        high = jnp.concatenate([target_rows(total, x, 1, i_dev) for x in range(4)], axis=0)
        keep_ref[0, block] = jnp.where(here == 0, low, high)
        code, level = encode(jnp.where(here == 0, high, low))
        send_ref[0, block * size : (block + 1) * size, :] = code
        levels.append(level)
    send_ref[0, len(sums) * size :, :] = level_rows(levels)


def own_z_part(z_dev, lam_rows, panel, recv, first, width):
    rows, depth = lam_rows.shape
    tiles, offset = width // TILE, first // TILE
    blocks = TILE // LANES
    size = blocks * (rows // 2) + SCALE_ROWS
    return pl.pallas_call(
        own_z_kernel,
        grid=(tiles,),
        in_specs=[
            pl.BlockSpec(memory_space=pltpu.SMEM),
            pl.BlockSpec((rows, depth), lambda t: (0, 0)),
            pl.BlockSpec((depth, TILE), lambda t: (0, t + offset)),
            pl.BlockSpec((1,) + recv.shape[1:], lambda t: (t, 0, 0)),
        ],
        out_specs=[
            pl.BlockSpec((1, size, LANES), lambda t: (t, 0, 0)),
            pl.BlockSpec((1, blocks, rows // 2, LANES), lambda t: (t, 0, 0, 0)),
        ],
        out_shape=[
            jax.ShapeDtypeStruct((tiles, size, LANES), jnp.int16),
            jax.ShapeDtypeStruct((tiles, blocks, rows // 2, LANES), jnp.float32),
        ],
        compiler_params=params(),
        cost_estimate=cost(rows, depth, width),
        name="own_z_part",
    )(z_dev, lam_rows, panel, recv)


def own_x_kernel(lam_ref, panel_ref, recv_ref, send_ref):
    i_dev = lam_ref.shape[0] // 64
    sums = own_sum(lam_ref, panel_ref, recv_ref)
    size = 2 * i_dev * 8
    for x in range(4):
        levels = []
        for block, total in enumerate(sums):
            rows = jnp.concatenate([target_rows(total, x, z, i_dev) for z in range(2)], axis=0)
            code, level = encode(rows)
            send_ref[x, 0, block * size : (block + 1) * size, :] = code
            levels.append(level)
        send_ref[x, 0, len(sums) * size :, :] = level_rows(levels)


def own_x_part(lam_rows, panel, recv, first, width):
    rows, depth = lam_rows.shape
    tiles, offset = width // TILE, first // TILE
    blocks = TILE // LANES
    size = blocks * (rows // 4) + SCALE_ROWS
    return pl.pallas_call(
        own_x_kernel,
        grid=(tiles,),
        in_specs=[
            pl.BlockSpec((rows, depth), lambda t: (0, 0)),
            pl.BlockSpec((depth, TILE), lambda t: (0, t + offset)),
            pl.BlockSpec((1,) + recv.shape[1:], lambda t: (t, 0, 0)),
        ],
        out_specs=pl.BlockSpec((4, 1, size, LANES), lambda t: (0, t, 0, 0)),
        out_shape=jax.ShapeDtypeStruct((4, tiles, size, LANES), jnp.int16),
        compiler_params=params(),
        cost_estimate=cost(rows, depth, width),
        name="own_x_part",
    )(lam_rows, panel, recv)


def merge_z_kernel(keep_ref, recv_ref, send_ref):
    tiles, blocks, rows, _ = keep_ref.shape
    owner = rows // 4
    levels = [[] for _ in range(4)]
    for tile in range(tiles):
        got = read_levels(recv_ref[tile, blocks * rows :, :])
        for block in range(blocks):
            at = (tile * blocks + block) * owner
            for x in range(4):
                part = slice(block * rows + x * owner, block * rows + (x + 1) * owner)
                total = keep_ref[tile, block, x * owner : (x + 1) * owner, :] + decode(
                    recv_ref[tile, part, :], got[block : block + 1, :]
                )
                code, level = encode(total)
                send_ref[x, at : at + owner, :] = code
                levels[x].append(level)
    for x in range(4):
        send_ref[x, tiles * blocks * owner :, :] = level_rows(levels[x])


def merge_z(keep, recv):
    tiles, blocks, rows, _ = keep.shape
    size = tiles * blocks * (rows // 4) + SCALE_ROWS
    return pl.pallas_call(
        merge_z_kernel,
        out_shape=jax.ShapeDtypeStruct((4, size, LANES), jnp.int16),
        compiler_params=params(),
        cost_estimate=cost(0, 0, 0, 6 * keep.size + 2 * recv.size),
        name="merge_z",
    )(keep, recv)


def merge_x_kernel(z_ref, recv_ref, send_ref, keep_ref):
    sources, tiles, size, _ = recv_ref.shape
    blocks = TILE // LANES
    rows = (size - SCALE_ROWS) // blocks
    owner = rows // 2
    here = z_ref[0]
    levels = []
    for tile in range(tiles):
        got = [read_levels(recv_ref[s, tile, blocks * rows :, :]) for s in range(sources)]
        for block in range(blocks):
            at = tile * blocks + block
            total = sum(
                decode(recv_ref[s, tile, block * rows : (block + 1) * rows, :], got[s][block : block + 1, :])
                for s in range(sources)
            )
            low, high = total[:owner, :], total[owner:, :]
            keep_ref[at] = jnp.where(here == 0, low, high)
            code, level = encode(jnp.where(here == 0, high, low))
            send_ref[at * owner : (at + 1) * owner, :] = code
            levels.append(level)
    send_ref[tiles * blocks * owner :, :] = level_rows(levels)


def merge_x(z_dev, recv):
    sources, tiles, size, _ = recv.shape
    blocks = TILE // LANES
    owner = (size - SCALE_ROWS) // blocks // 2
    return pl.pallas_call(
        merge_x_kernel,
        in_specs=[pl.BlockSpec(memory_space=pltpu.SMEM), pl.BlockSpec(memory_space=pltpu.VMEM)],
        out_shape=[
            jax.ShapeDtypeStruct((tiles * blocks * owner + SCALE_ROWS, LANES), jnp.int16),
            jax.ShapeDtypeStruct((tiles * blocks, owner, LANES), jnp.float32),
        ],
        compiler_params=params(),
        cost_estimate=cost(0, 0, 0, 2 * recv.size),
        name="merge_x",
    )(z_dev, recv)


def finish_kernel(z_recv_ref, x_keep_ref, x_recv_ref, cycle_ref, out_ref):
    sources = z_recv_ref.shape[0]
    x_blocks, rows, _ = x_keep_ref.shape
    z_blocks = (z_recv_ref.shape[1] - SCALE_ROWS) // rows
    i_dev = rows // 8
    z_levels = [read_levels(z_recv_ref[s, z_blocks * rows :, :]) for s in range(sources)]
    x_levels = read_levels(x_recv_ref[x_blocks * rows :, :])
    halves = BW // LANES

    def ladder(block):
        if block < z_blocks:
            part = slice(block * rows, (block + 1) * rows)
            return sum(decode(z_recv_ref[s, part, :], z_levels[s][block : block + 1, :]) for s in range(sources))
        block -= z_blocks
        part = slice(block * rows, (block + 1) * rows)
        return x_keep_ref[block] + decode(x_recv_ref[part, :], x_levels[block : block + 1, :])

    for half in range(halves):
        for group in range(AW // 8):
            totals = [ladder((group * 8 + a) * halves + half) for a in range(8)]
            for i in range(i_dev):
                stack = jnp.stack([total[i * 8 : (i + 1) * 8, :] for total in totals], axis=0)
                turned = jnp.swapaxes(stack, 0, 1)
                at = pl.ds(i * AW + group * 8, 8)
                for jj in range(8):
                    lanes = pl.ds(jj * BW + half * LANES, LANES)
                    out_ref[at, lanes] = turned[jj] + cycle_ref[at, lanes]


def finish(z_recv, x_keep, x_recv, cycle):
    return pl.pallas_call(
        finish_kernel,
        out_shape=jax.ShapeDtypeStruct(cycle.shape, jnp.float32),
        compiler_params=params(),
        cost_estimate=cost(0, 0, 0, 2 * z_recv.size + 6 * x_keep.size + 8 * cycle.size),
        name="finish",
    )(z_recv, x_keep, x_recv, cycle)


def cycle_kernel(kc_ref, jb_ref, amp_ref, packed_ref, spread_ref, out_ref):
    depth = packed_ref.shape[0]
    step = depth // 5
    total = jnp.zeros(out_ref.shape, jnp.float32)
    for part in range(5):
        rows = pl.ds(part * step, step)
        wide = jnp.dot(packed_ref[rows, :], spread_ref[...], preferred_element_type=jnp.float32)
        allowed = kc_ref[rows, :] == jb_ref[...]
        masked = jnp.where(allowed, wide, 0.0).astype(jnp.bfloat16)
        total += jnp.dot(amp_ref[:, part * step : (part + 1) * step], masked, preferred_element_type=jnp.float32)
    out_ref[...] = total


def cycle_term(kc_irrep, jb_irrep, amp, packed, spread):
    rows, depth = amp.shape
    pairs = packed.shape[1] // LANES
    width = spread.shape[1]
    return pl.pallas_call(
        cycle_kernel,
        grid=(pairs,),
        in_specs=[
            pl.BlockSpec((depth, 1), lambda t: (0, 0)),
            pl.BlockSpec((1, width), lambda t: (0, t)),
            pl.BlockSpec((rows, depth), lambda t: (0, 0)),
            pl.BlockSpec((depth, LANES), lambda t: (0, t)),
            pl.BlockSpec((LANES, width), lambda t: (0, 0)),
        ],
        out_specs=pl.BlockSpec((rows, width), lambda t: (0, t)),
        out_shape=jax.ShapeDtypeStruct((rows, pairs * width), jnp.float32),
        compiler_params=params(),
        cost_estimate=cost(2 * rows, depth, pairs * width),
        name="cycle_term",
    )(kc_irrep[:, None], jb_irrep[None, :], amp, packed, spread)


def swap(value, axis):
    return lax.ppermute(value, axis, [(0, 1), (1, 0)])


def labels_of(occ_irrep, virt_irrep):
    vir_count = lax.axis_size(VIR)
    j_width = JW // vir_count
    j_irrep = lax.dynamic_slice_in_dim(occ_irrep, lax.axis_index(VIR) * j_width, j_width, 0)
    jb_irrep = (j_irrep[:, None] ^ virt_irrep[None, :]).reshape(-1)
    kc_irrep = (occ_irrep[:, None] ^ virt_irrep[None, :PAN]).reshape(-1)
    return kc_irrep, jb_irrep


def device_step(packed_path, lam, ladder_int, cycle_amp, cycle_int, occ_irrep, virt_irrep):
    kc_irrep, jb_irrep = labels_of(occ_irrep, virt_irrep)
    if packed_path:
        mine = lax.dynamic_slice_in_dim(kc_irrep, lax.axis_index(OCC) * cycle_int.shape[0], cycle_int.shape[0], 0)
        place = jnp.arange(BW) - jnp.sum(virt_irrep[None, :] < virt_irrep[:, None], axis=1)
        one_hot = (jnp.arange(SEGMENT)[:, None] == place[None, :]).astype(jnp.bfloat16)
        group = LANES // SEGMENT
        spread = jnp.kron(jnp.eye(group, dtype=jnp.bfloat16), one_hot)
        masked = jnp.where(mine[:, None] == jb_irrep[None, :], cycle_int, jnp.zeros((), cycle_int.dtype))
        masked = masked.reshape(-1, group * BW)
        packed = jnp.dot(masked, spread.T, preferred_element_type=jnp.float32).astype(jnp.bfloat16)
        packed = packed.reshape(cycle_int.shape[0], -1)
        gathered = lax.all_gather(packed, OCC, axis=0, tiled=True)
    else:
        gathered = lax.all_gather(cycle_int, OCC, axis=0, tiled=True)

    rows, depth = lam.shape
    halves = lam.reshape(rows // 16, 2, 8, depth)
    core = lax.axis_index("core")
    z_dev = lax.axis_index("z_hi").astype(jnp.int32).reshape(1)
    other = lax.dynamic_index_in_dim(halves, 1 - core, 1, keepdims=False).reshape(rows // 2, depth)
    own = lax.dynamic_index_in_dim(halves, core, 1, keepdims=False).reshape(rows // 2, depth)
    columns = ladder_int.shape[1]
    x_columns = columns - Z_COLUMNS

    z_swapped = swap(partner_part(other, ladder_int, 0, Z_COLUMNS), "core")
    x_swapped = swap(partner_part(other, ladder_int, Z_COLUMNS, x_columns), "core")
    z_send, z_keep = own_z_part(z_dev, own, ladder_int, z_swapped, 0, Z_COLUMNS)
    z_recv = swap(z_send, "z_hi")
    x_send = own_x_part(own, ladder_int, x_swapped, Z_COLUMNS, x_columns)
    x_recv = lax.all_to_all(x_send, "x", 0, 0)
    z_second = lax.all_to_all(merge_z(z_keep, z_recv), "x", 0, 0)
    x_second_send, x_keep = merge_x(z_dev, x_recv)
    x_second = swap(x_second_send, "z_hi")

    if packed_path:
        cycle = cycle_term(kc_irrep, jb_irrep, cycle_amp, gathered, spread)
    else:
        allowed = kc_irrep[:, None] == jb_irrep[None, :]
        masked = jnp.where(allowed, gathered, jnp.zeros((), gathered.dtype))
        cycle = jnp.dot(cycle_amp, masked, preferred_element_type=jnp.float32)
    return finish(z_second, x_keep, x_second, cycle)


def per_device(lam, ladder_int, cycle_amp, cycle_int, occ_irrep, virt_irrep):
    longest = jnp.max(jnp.sum(virt_irrep[:, None] == jnp.arange(8)[None, :], axis=0))
    return lax.cond(
        longest <= SEGMENT,
        functools.partial(device_step, True),
        functools.partial(device_step, False),
        lam,
        ladder_int,
        cycle_amp,
        cycle_int,
        occ_irrep,
        virt_irrep,
    )


def solution(mesh):
    fine = Mesh(mesh.devices.reshape(2, 4, 4, 2, 2), ("z_lo", "y", "x", "z_hi", "core"))
    return jax.shard_map(
        per_device,
        mesh=fine,
        in_specs=(P(OCC, VIR), P(VIR, None), P(OCC, None), P(OCC, VIR), P(), P()),
        out_specs=P(OCC, VIR),
        check_vma=False,
    )
```

time: 312 us -> 132 us (0.42)
  waiting for transfers between devices: 244 us -> 23.6 us
  Pallas kernels: 0 us -> 54.2 us
  matrix products: 30.4 us -> 0.59 us
  starting transfers between devices: 0.05 us -> 16.7 us
  local copies, waits for them, and re-layouts: 21.8 us -> 14.9 us
  other arithmetic: 0.16 us -> 5.95 us
    reduce_scatter x1 -> x0, waiting for transfers between devices: 243 us -> none  [per_device(): lax.psum_scatter(jnp.einsum('ijk,kn->jin', lam_blocks, ladder_int, prefer...]
    pallas_call x0 -> x8, Pallas kernels: none -> 54.2 us  [the longest x2 17.2 us: partner_part(): pl.pallas_call(partner_kernel, grid=(tiles,), in_specs=[pl.BlockSpec((row...]
    dot_general x2 -> x1, matrix products: 30.4 us -> 0.59 us  [device_step(): jnp.dot(masked, spread.T, preferred_element_type=jnp.float32)]
    ppermute x0 -> x4, waiting for transfers between devices: none -> 23.6 us  [swap(): return lax.ppermute(value, axis, [(0, 1), (1, 0)])]
    transpose x1 -> x0, local copies, waits for them, and re-layouts: 17.7 us -> none  [per_device(): jnp.einsum('ijk,kn->jin', lam_blocks, ladder_int, preferred_element_type=...]
    all_to_all x0 -> x2, starting transfers between devices: none -> 8.87 us  [the longest x1 4.52 us: device_step(): z_second = lax.all_to_all(merge_z(z_keep, z_recv), 'x', 0, 0)]
    ppermute x0 -> x4, starting transfers between devices: none -> 7.64 us  [swap(): return lax.ppermute(value, axis, [(0, 1), (1, 0)])]
    reshape x2 -> x3, local copies, waits for them, and re-layouts: 2.16 us -> 6.24 us  [the longest x1 4.22 us: device_step(): lax.dynamic_index_in_dim(halves, 1 - core, 1, keepdims=False)]
  transfers between devices with their start and end apart: 2 -> 7, of which waited for: 1 -> 1; matrix products, arithmetic and copies ran while one was open for 1% -> 5% of each run, Pallas kernels for 0% -> 40%
where the time goes in v1:
time: 132 us; the launch traced here: 130 us
  Pallas kernels  54.2 us (41%)
  waiting for transfers between devices  23.6 us (18%)
  starting transfers between devices  16.7 us (13%)
  local copies, waits for them, and re-layouts  14.9 us (11%)
  between operations  14.1 us (11%)
  other arithmetic  5.95 us (5%)
    ppermute x4, waiting for transfers between devices, swap(): return lax.ppermute(value, axis, [(0, 1), (1, 0)])  23.6 us
    pallas_call x2, Pallas kernels, partner_part(): pl.pallas_call(partner_kernel, grid=(tiles,), in_specs=[pl.BlockSpec((row...  17.2 us
    pallas_call x1, Pallas kernels, cycle_term(): pl.pallas_call(cycle_kernel, grid=(pairs,), in_specs=[pl.BlockSpec((depth...  10.1 us
    pallas_call x1, Pallas kernels, own_x_part(): pl.pallas_call(own_x_kernel, grid=(tiles,), in_specs=[pl.BlockSpec((rows,...  9.04 us
    pallas_call x1, Pallas kernels, own_z_part(): pl.pallas_call(own_z_kernel, grid=(tiles,), in_specs=[pl.BlockSpec(memory...  8.79 us
    ppermute x4, starting transfers between devices, swap(): return lax.ppermute(value, axis, [(0, 1), (1, 0)])  7.64 us
    all_to_all x1, starting transfers between devices, device_step(): z_second = lax.all_to_all(merge_z(z_keep, z_recv), 'x', 0, 0)  4.52 us
    all_to_all x1, starting transfers between devices, device_step(): x_recv = lax.all_to_all(x_send, 'x', 0, 0)  4.36 us
  transfers between devices with their start and end apart: 7, of which 1 were waited for; matrix products, arithmetic and copies ran while one was open for 5% of the time, Pallas kernels for 40%

profile of v1, /device:TPU:0, one launch (start us, length us, event | category | flops | bytes accessed | tf_op | source)
XLA Modules:
  0.0 130.5 jit_solution(6212143284871042240)
XLA Ops:
  6.5 0.8 convert_reduce_fusion.1
  7.3 0.6 reduce_max.9
  8.6 114.0 %conditional.1 = (f32[128,2048]{1,0:T(8,128)S(1)}) conditional(s32[]{:T(128)} %convert_element_type.27, (bf16[1024,1792]{1,0:T(8,128)(2,1)}, bf16[1792,4096]{1,0:T(8,128)(2,1)}, s32[200]{0:T(256)}, s32[256]{0:T(256)}, bf16[400,2048]{1,0:T(8,128)(2,1)}, /*index=5*/bf16[128,3200]{1,0:T(8,128)(2,1)}) %tuple.11, (bf16[1024,1792]{1,0:T(8,128)(2,1)}, ...), branch_computations={%region_2.3_spmd, %region_3.5_spmd} | conditional | flops 18599686144 | bytes 172273600 | solution.py:395
  8.6 0.2 all-gather.5.cloned.1.call-start
  8.9 0.7 slice.5
  9.6 0.9 convert_reduce_fusion
  10.5 0.8 dynamic_slice.20
  11.3 0.7 xor_bitcast_fusion.1
  12.1 0.2 broadcast_multiply_fusion
  12.3 0.0 copy-start.9
  12.3 0.8 broadcast_xor_fusion.1
  13.1 0.1 xor.92
  13.2 0.1 dynamic_slice.21
  13.2 1.9 %compare_select_fusion.4 = bf16[400,2048]{1,0:T(8,128)(2,1)S(1)} fusion(bf16[400,2048]{1,0:T(8,128)(2,1)} %get-tuple-element.51, s32[2048]{0:T(1024)S(1)} %bitcast.43, s32[400]{0:T(512)S(1)} %dynamic_slice.21), kind=kLoop, calls=%fused_computation.11 | loop fusion | flops 1638400 | bytes 3286592 | tf_op jit(solution)/shard_map/cond/branch_1_fun/jit(_where)/select_n | solution.py:357
  15.1 1.0 reshape.177
  16.1 0.0 copy-done.9
  16.2 0.6 convolution_convert_fusion
  16.7 1.0 reshape.178
  17.7 0.0 all-gather.5.cloned.1.call-update
  17.8 4.2 %dynamic-slice_bitcast_fusion.2 = (bf16[512,1792]{1,0:T(8,128)(2,1)}, bf16[512,1792]{1,0:T(8,128)(2,1)}) fusion(bf16[64,2,8,1792]{3,2,1,0:T(8,128)(2,1)} %bitcast.39, s32[]{:T(128)S(6)} %select_n.26, s32[]{:T(128)S(6)} %select_n.25), kind=kLoop, calls=%fused_computation.13 | loop fusion | bytes 7340040 | tf_op jit(solution)/shard_map/cond/branch_1_fun/reshape | solution.py:369
  22.0 8.6 %partner_part.7 = s16[4,2064,128]{2,1,0:T(8,128)(2,1)} custom-call(bf16[512,1792]{1,0:T(8,128)(2,1)} %get-tuple-element.55.lam_ref, bf16[1792,4096]{1,0:T(8,128)(2,1)} %get-tuple-element.43.panel_ref), custom_call_target="tpu_custom_call" | custom-call | flops 3758096384 | bytes 9175040 | tf_op jit(solution)/shard_map/cond/branch_1_fun/partner_part/pallas_call | solution.py:79
  30.6 0.0 collective-permute-start.6
  30.6 8.6 %partner_part.6 = s16[4,2064,128]{2,1,0:T(8,128)(2,1)} custom-call(bf16[512,1792]{1,0:T(8,128)(2,1)} %get-tuple-element.55.lam_ref, bf16[1792,4096]{1,0:T(8,128)(2,1)} %get-tuple-element.43.panel_ref), custom_call_target="tpu_custom_call" | custom-call | flops 3758096384 | bytes 9175040 | tf_op jit(solution)/shard_map/cond/branch_1_fun/partner_part/pallas_call | solution.py:79
  39.2 0.5 collective-permute-start.4
  39.7 0.0 collective-permute-done.6.recv_ref
  39.7 1.3 copy-done.5
  41.0 9.0 %own_x_part.3 = s16[4,4,528,128]{3,2,1,0:T(8,128)(2,1)} custom-call(bf16[512,1792]{1,0:T(8,128)(2,1)} %get-tuple-element.56.lam_ref, bf16[1792,4096]{1,0:T(8,128)(2,1)} %get-tuple-element.43.panel_ref, s16[4,2064,128]{2,1,0:T(8,128)(2,1)} %copy-done.5), custom_call_target="tpu_custom_call" | custom-call | flops 3758096384 | bytes 9175040 | tf_op jit(solution)/shard_map/cond/branch_1_fun/own_x_part/pallas_call | solution.py:174
  50.1 4.4 %all-to-all-start.3 = ((s16[4,4,528,128]{3,2,1,0:T(8,128)(2,1)}), s16[4,4,528,128]{3,2,1,0:T(8,128)(2,1)S(1)}, u32[]{:S(2)}, u32[]{:S(2)}) async-start(s16[4,4,528,128]{3,2,1,0:T(8,128)(2,1)} %own_x_part.3), calls=%async_computation.3 | async-start | bytes 4325376 | tf_op jit(solution)/shard_map/cond/branch_1_fun/all_to_all | solution.py:379
  54.4 0.0 collective-permute-done.4.recv_ref
  54.4 8.8 %own_z_part.3 = (s16[4,1040,128]{2,1,0:T(8,128)(2,1)}, f32[4,4,256,128]{3,2,1,0:T(8,128)}) custom-call(s32[1]{0:T(128)} %bitcast.5.z_ref, bf16[512,1792]{1,0:T(8,128)(2,1)} %get-tuple-element.56.lam_ref, bf16[1792,4096]{1,0:T(8,128)(2,1)} %get-tuple-element.43.panel_ref, s16[4,2064,128]{2,1,0:T(8,128)(2,1)} %collective-permute-done.4.recv_ref), custom_call_target="tpu_custom_call" | custom-call | flops 3758096384 | bytes 9175040 | tf_op jit(solution)/shard_map/cond/branch_1_fun/own_z_part/pallas_call | solution.py:132
  63.2 3.9 %collective-permute-start.5 = (s16[4,1040,128]{2,1,0:T(8,128)(2,1)}, s16[4,1040,128]{2,1,0:T(8,128)(2,1)S(1)}, u32[]{:S(2)}, u32[]{:S(2)}) collective-permute-start(s16[4,1040,128]{2,1,0:T(8,128)(2,1)} %get-tuple-element.45), channel_id=1, source_target_pairs={{0,2},{2,0},{1,3},{3,1},{4,6},{6,4},{5,7},{7,5},{8,10},{10,8},{9,1... | collective-permute-start | bytes 3194888 | tf_op jit(solution)/shard_map/cond/branch_1_fun/ppermute | solution.py:337
  67.1 23.6 %collective-permute-done.5.recv_ref = s16[4,1040,128]{2,1,0:T(8,128)(2,1)S(1)} collective-permute-done((s16[4,1040,128]{2,1,0:T(8,128)(2,1)}, s16[4,1040,128]{2,1,0:T(8,128)(2,1)S(1)}, u32[]{:S(2)}, u32[]{:S(2)}) %collective-permute-start.5) | collective-permute-done | bytes 1064992 | tf_op jit(solution)/shard_map/cond/branch_1_fun/ppermute | solution.py:337
  90.7 1.0 copy-done.7
  91.7 3.5 %merge_z.3 = s16[4,1040,128]{2,1,0:T(8,128)(2,1)} custom-call(f32[4,4,256,128]{3,2,1,0:T(8,128)} %get-tuple-element.44.keep_ref, s16[4,1040,128]{2,1,0:T(8,128)(2,1)} %copy-done.7), custom_call_target="tpu_custom_call" | custom-call | bytes 4210688 | tf_op jit(solution)/shard_map/cond/branch_1_fun/merge_z/pallas_call | solution.py:213
  95.2 0.0 all-to-all-done.3.recv_ref
  95.2 4.5 %all-to-all-start.2 = ((s16[4,1040,128]{2,1,0:T(8,128)(2,1)}), s16[4,1040,128]{2,1,0:T(8,128)(2,1)S(1)}, u32[]{:S(2)}, u32[]{:S(2)}) async-start(s16[4,1040,128]{2,1,0:T(8,128)(2,1)} %merge_z.3), calls=%async_computation.2 | async-start | bytes 2129920 | tf_op jit(solution)/shard_map/cond/branch_1_fun/all_to_all | solution.py:380
  99.7 2.1 %xor.94.kc_ref = s32[3200,1]{1,0:T(8,128)} reshape(s32[200,16]{1,0:T(8,128)S(1)} %broadcast_xor_fusion.1) | data formatting | bytes 25600 | tf_op jit(solution)/shard_map/cond/branch_1_fun/xor | solution.py:345
  101.8 0.6 copy.32
  102.4 3.2 %merge_x.3 = (s16[1040,128]{1,0:T(8,128)(2,1)}, f32[16,64,128]{2,1,0:T(8,128)}) custom-call(s32[1]{0:T(128)} %bitcast.5.z_ref, s16[4,4,528,128]{3,2,1,0:T(8,128)(2,1)} %copy-done.1), custom_call_target="tpu_custom_call" | custom-call | bytes 2162688 | tf_op jit(solution)/shard_map/cond/branch_1_fun/merge_x/pallas_call | solution.py:249
  105.6 3.2 %collective-permute-start.7 = (s16[1040,128]{1,0:T(8,128)(2,1)}, s16[1040,128]{1,0:T(8,128)(2,1)S(1)}, u32[]{:S(2)}, u32[]{:S(2)}) collective-permute-start(s16[1040,128]{1,0:T(8,128)(2,1)} %get-tuple-element.47), channel_id=1, source_target_pairs={{0,2},{2,0},{1,3},{3,1},{4,6},{6,4},{5,7},{7,5},{8,10},{10,8},{9,1... | collective-permute-start | bytes 798728 | tf_op jit(solution)/shard_map/cond/branch_1_fun/ppermute | solution.py:337
  108.9 10.1 %cycle_term.1.cycle_ref = f32[128,2048]{1,0:T(8,128)} custom-call(s32[3200,1]{1,0:T(8,128)} %xor.94.kc_ref, s32[1,2048]{1,0:T(1,128)} %bitcast.45, bf16[128,3200]{1,0:T(8,128)(2,1)} %get-tuple-element.50.amp_ref, bf16[3200,512]{1,0:T(8,128)(2,1)} %all-gather.5.cloned.1.call-done.packed_ref, bf16[128,512]{1,0:T(8,128)(2,1)} %bitcast.41), custom_call_target="tpu_custom_call" | custom-call | flops 3355443200 | bytes 14745600 | tf_op jit(solution)/shard_map/cond/branch_1_fun/cycle_term/pallas_call | solution.py:318
  119.0 0.0 all-to-all-done.2.z_recv_ref
  119.0 0.0 collective-permute-done.7.x_recv_ref
  119.0 1.0 copy-done.2
  120.0 0.1 copy-done.10
  120.1 2.3 %finish.3 = f32[128,2048]{1,0:T(8,128)S(1)} custom-call(s16[4,1040,128]{2,1,0:T(8,128)(2,1)} %copy-done.2, f32[16,64,128]{2,1,0:T(8,128)} %get-tuple-element.46.x_keep_ref, s16[1040,128]{1,0:T(8,128)(2,1)} %copy-done.10, f32[128,2048]{1,0:T(8,128)} %cycle_term.1.cycle_ref), custom_call_target="tpu_custom_call" | custom-call | bytes 3948544 | tf_op jit(solution)/shard_map/cond/branch_1_fun/finish/pallas_call | solution.py:292
  122.7 0.0 copy-start.8
  122.7 1.0 copy-done.8
  (12 shorter events, 0.1 us)
Async XLA Ops:
  8.6 100.2 %all-gather.5.cloned.1.call-start = ((), (), s32[]{:S(2)}) async-start(), calls=%async_computation.5 | async-start | bytes 3686400 | tf_op jit(solution)/shard_map/cond/branch_1_fun/all_gather | solution.py:361
  12.3 3.9 %copy-start.9 = (bf16[16,8,2,256]{3,1,2,0:T(8,128)(2,1)}, bf16[16,8,2,256]{3,1,2,0:T(8,128)(2,1)S(1)}, u32[]{:S(2)}) copy-start(bf16[16,8,2,256]{3,1,2,0:T(8,128)(2,1)S(1)} %copy.34) | copy-start | bytes 393220 | tf_op jit(solution)/shard_map/cond
  30.6 9.1 %collective-permute-start.6 = (s16[4,2064,128]{2,1,0:T(8,128)(2,1)}, s16[4,2064,128]{2,1,0:T(8,128)(2,1)S(1)}, u32[]{:S(2)}, u32[]{:S(2)}) collective-permute-start(s16[4,2064,128]{2,1,0:T(8,128)(2,1)} %partner_part.7), channel_id=1, source_target_pairs={{0,1},{1,0},{2,3},{3,2},{4,5},{5,4},{6,7},{7,6},{8,9},{9,8},{10,11... | collective-permute-start | bytes 6340616 | tf_op jit(solution)/shard_map/cond/branch_1_fun/ppermute | solution.py:337
  39.2 15.2 %collective-permute-start.4 = (s16[4,2064,128]{2,1,0:T(8,128)(2,1)}, s16[4,2064,128]{2,1,0:T(8,128)(2,1)}, u32[]{:S(2)}, u32[]{:S(2)}) collective-permute-start(s16[4,2064,128]{2,1,0:T(8,128)(2,1)} %partner_part.6), channel_id=1, source_target_pairs={{0,1},{1,0},{2,3},{3,2},{4,5},{5,4},{6,7},{7,6},{8,9},{9,8},{10,11... | collective-permute-start | bytes 6340616 | tf_op jit(solution)/shard_map/cond/branch_1_fun/ppermute | solution.py:337
  39.7 1.3 %copy-start.5 = (s16[4,2064,128]{2,1,0:T(8,128)(2,1)}, s16[4,2064,128]{2,1,0:T(8,128)(2,1)S(1)}, u32[]{:S(2)}) copy-start(s16[4,2064,128]{2,1,0:T(8,128)(2,1)S(1)} %collective-permute-done.6.recv_ref) | copy-start | bytes 6340612 | tf_op jit(solution)/shard_map/cond
  50.1 45.2 %all-to-all-start.3 = ((s16[4,4,528,128]{3,2,1,0:T(8,128)(2,1)}), s16[4,4,528,128]{3,2,1,0:T(8,128)(2,1)S(1)}, u32[]{:S(2)}, u32[]{:S(2)}) async-start(s16[4,4,528,128]{3,2,1,0:T(8,128)(2,1)} %own_x_part.3), calls=%async_computation.3 | async-start | bytes 4325376 | tf_op jit(solution)/shard_map/cond/branch_1_fun/all_to_all | solution.py:379
  63.2 27.5 %collective-permute-start.5 = (s16[4,1040,128]{2,1,0:T(8,128)(2,1)}, s16[4,1040,128]{2,1,0:T(8,128)(2,1)S(1)}, u32[]{:S(2)}, u32[]{:S(2)}) collective-permute-start(s16[4,1040,128]{2,1,0:T(8,128)(2,1)} %get-tuple-element.45), channel_id=1, source_target_pairs={{0,2},{2,0},{1,3},{3,1},{4,6},{6,4},{5,7},{7,5},{8,10},{10,8},{9,1... | collective-permute-start | bytes 3194888 | tf_op jit(solution)/shard_map/cond/branch_1_fun/ppermute | solution.py:337
  90.7 1.0 copy-start.7
  95.2 7.2 %copy-start.1 = (s16[4,4,528,128]{3,2,1,0:T(8,128)(2,1)}, s16[4,4,528,128]{3,2,1,0:T(8,128)(2,1)S(1)}, u32[]{:S(2)}) copy-start(s16[4,4,528,128]{3,2,1,0:T(8,128)(2,1)S(1)} %all-to-all-done.3.recv_ref) | copy-start | bytes 6488068 | tf_op jit(solution)/shard_map/cond
  95.2 23.8 %all-to-all-start.2 = ((s16[4,1040,128]{2,1,0:T(8,128)(2,1)}), s16[4,1040,128]{2,1,0:T(8,128)(2,1)S(1)}, u32[]{:S(2)}, u32[]{:S(2)}) async-start(s16[4,1040,128]{2,1,0:T(8,128)(2,1)} %merge_z.3), calls=%async_computation.2 | async-start | bytes 2129920 | tf_op jit(solution)/shard_map/cond/branch_1_fun/all_to_all | solution.py:380
  105.6 13.4 %collective-permute-start.7 = (s16[1040,128]{1,0:T(8,128)(2,1)}, s16[1040,128]{1,0:T(8,128)(2,1)S(1)}, u32[]{:S(2)}, u32[]{:S(2)}) collective-permute-start(s16[1040,128]{1,0:T(8,128)(2,1)} %get-tuple-element.47), channel_id=1, source_target_pairs={{0,2},{2,0},{1,3},{3,1},{4,6},{6,4},{5,7},{7,5},{8,10},{10,8},{9,1... | collective-permute-start | bytes 798728 | tf_op jit(solution)/shard_map/cond/branch_1_fun/ppermute | solution.py:337
  119.0 1.0 copy-start.2
  119.0 1.1 copy-start.10
  122.7 1.0 copy-start.8
Sparse Core Ops, SparseCore 0:
  17.9 47.0 all-gather.4

commit v2 on v0

v2 whole, which is shorter than its diff:
```python
import functools

import jax
import jax.numpy as jnp
from jax import lax
from jax.experimental import pallas as pl
from jax.experimental.pallas import tpu as pltpu
from jax.sharding import Mesh, PartitionSpec as P

PAN = 16
AW = 16
BW = 256
JW = 128
LANES = 128
HALVES = BW // LANES
SCALE_ROWS = 16
SEGMENT = 64
MIB = 1024 * 1024

VIR = ("x", "z_hi", "core")
OCC = ("z_lo", "y")
CHUNKS = (("x", 10, 5), ("z", 6, 2))
ORDER = ("P0", "P1", "O0", "O1", "C", "M0", "M1")
SCALE = 8


def encode(block):
    top = jnp.maximum(jnp.max(jnp.abs(block), axis=0, keepdims=True), 1e-30)
    level = jnp.ceil(jnp.log2(top) * 256.0) + 1.0
    step = jnp.exp2(level * (-1.0 / 256.0)) * 32767.0
    return jnp.round(block * step).astype(jnp.int32).astype(jnp.int16), level


def lane_block(value, block):
    return value[:, block * LANES : (block + 1) * LANES]


def decode(code, step):
    return code.astype(jnp.int32).astype(jnp.float32) * step


def level_rows(level):
    blocks = level.shape[1] // LANES
    rows = [lane_block(level, block) for block in range(blocks)]
    spare = jnp.zeros((1, LANES), jnp.float32)
    rows = jnp.concatenate(rows + [spare] * (SCALE_ROWS - blocks), axis=0)
    return rows.astype(jnp.int32).astype(jnp.int16)


def read_steps(block):
    level = block.astype(jnp.int32).astype(jnp.float32)
    return jnp.exp2(level * (1.0 / 256.0)) * (1.0 / 32767.0)


def params(mib):
    return pltpu.CompilerParams(vmem_limit_bytes=mib * MIB)


def in_hbm(value):
    return pltpu.with_memory_space_constraint(value, pltpu.HBM)


def in_vmem(value):
    return pltpu.with_memory_space_constraint(value, pltpu.VMEM)


def cost(rows, depth, columns, more=0):
    flops, moved = 2 * rows * depth * columns, 2 * (rows * depth + depth * columns) + more
    return pl.CostEstimate(flops=flops // SCALE, bytes_accessed=moved // SCALE + 1, transcendentals=0)


ANYWHERE = pl.BlockSpec(memory_space=pl.ANY)
SCALARS = pl.BlockSpec(memory_space=pltpu.SMEM)
WHOLE = pl.BlockSpec(memory_space=pltpu.VMEM)


def product(lam_rows, panel_ref):
    return jnp.dot(lam_rows, panel_ref[...], preferred_element_type=jnp.float32)


def partner_body(lam_rows, panel_ref, out_ref):
    rows = lam_rows.shape[0]
    acc = product(lam_rows, panel_ref)
    blocks = acc.shape[1] // LANES
    code, level = encode(acc)
    for block in range(blocks):
        out_ref[0, block * rows : (block + 1) * rows, :] = lane_block(code, block)
    out_ref[0, blocks * rows :, :] = level_rows(level)


def first_partner_kernel(lam_ref, panel_ref, _, out_ref, own_ref, other_ref):
    @pl.when(pl.program_id(0) == 0)
    def _select():
        here = lax.axis_index("core")
        for part in range(lam_ref.shape[0] // 32):
            rows = lam_ref[part * 32 : (part + 1) * 32, :].astype(jnp.float32)
            low = jnp.concatenate([rows[0:8], rows[16:24]], axis=0)
            high = jnp.concatenate([rows[8:16], rows[24:32]], axis=0)
            at = slice(part * 16, (part + 1) * 16)
            own_ref[at, :] = jnp.where(here == 0, low, high).astype(jnp.bfloat16)
            other_ref[at, :] = jnp.where(here == 0, high, low).astype(jnp.bfloat16)

    partner_body(other_ref[...], panel_ref, out_ref)


def first_partner_part(lam, panel, first, width, tile, after):
    rows, depth = lam.shape
    half = rows // 2
    tiles, offset = width // tile, first // tile
    size = tile // LANES * half + SCALE_ROWS
    return pl.pallas_call(
        first_partner_kernel,
        grid=(tiles,),
        in_specs=[
            pl.BlockSpec((rows, depth), lambda t: (0, 0)),
            pl.BlockSpec((depth, tile), lambda t: (0, t + offset)),
            ANYWHERE,
        ],
        out_specs=[
            pl.BlockSpec((1, size, LANES), lambda t: (t, 0, 0)),
            WHOLE,
            WHOLE,
        ],
        out_shape=[
            jax.ShapeDtypeStruct((tiles, size, LANES), jnp.int16),
            pltpu.VMEM((half, depth), jnp.bfloat16),
            pltpu.VMEM((half, depth), jnp.bfloat16),
        ],
        compiler_params=params(36),
        cost_estimate=cost(half, depth, width),
        name="partner_part",
    )(in_hbm(lam), in_hbm(panel), after)


def partner_kernel(lam_ref, panel_ref, _, out_ref):
    partner_body(lam_ref[...], panel_ref, out_ref)


def partner_part(lam_rows, panel, first, width, tile, after):
    rows, depth = lam_rows.shape
    tiles, offset = width // tile, first // tile
    size = tile // LANES * rows + SCALE_ROWS
    return pl.pallas_call(
        partner_kernel,
        grid=(tiles,),
        in_specs=[
            WHOLE,
            pl.BlockSpec((depth, tile), lambda t: (0, t + offset)),
            ANYWHERE,
        ],
        out_specs=pl.BlockSpec((1, size, LANES), lambda t: (t, 0, 0)),
        out_shape=jax.ShapeDtypeStruct((tiles, size, LANES), jnp.int16),
        compiler_params=params(20),
        cost_estimate=cost(rows, depth, width),
        name="partner_part",
    )(in_vmem(lam_rows), panel, after)


def own_sum(lam_ref, panel_ref, recv_ref):
    rows = lam_ref.shape[0]
    acc = product(lam_ref[...], panel_ref)
    blocks = acc.shape[1] // LANES
    tile = pl.program_id(0)
    steps = read_steps(recv_ref[tile, blocks * rows :, :])
    got = [
        decode(recv_ref[tile, block * rows : (block + 1) * rows, :], steps[block : block + 1, :])
        for block in range(blocks)
    ]
    return acc + jnp.concatenate(got, axis=1)


def target_rows(total, x_dev, z_dev, i_dev):
    pieces = [total[(i * 8 + x_dev * 2 + z_dev) * 8 : (i * 8 + x_dev * 2 + z_dev) * 8 + 8, :] for i in range(i_dev)]
    return jnp.concatenate(pieces, axis=0)


def own_z_kernel(lam_ref, panel_ref, recv_ref, _, send_ref, keep_ref):
    i_dev = lam_ref.shape[0] // 64
    here = lax.axis_index("z_hi")
    total = own_sum(lam_ref, panel_ref, recv_ref)
    blocks = total.shape[1] // LANES
    size = 4 * i_dev * 8
    low = jnp.concatenate([target_rows(total, x, 0, i_dev) for x in range(4)], axis=0)
    high = jnp.concatenate([target_rows(total, x, 1, i_dev) for x in range(4)], axis=0)
    keep = jnp.where(here == 0, low, high)
    code, level = encode(jnp.where(here == 0, high, low))
    for block in range(blocks):
        keep_ref[0, block] = lane_block(keep, block)
        send_ref[0, block * size : (block + 1) * size, :] = lane_block(code, block)
    send_ref[0, blocks * size :, :] = level_rows(level)


def own_z_part(lam_rows, panel, recv, first, width, tile, after):
    rows, depth = lam_rows.shape
    tiles, offset = width // tile, first // tile
    blocks = tile // LANES
    size = blocks * (rows // 2) + SCALE_ROWS
    return pl.pallas_call(
        own_z_kernel,
        grid=(tiles,),
        in_specs=[
            pl.BlockSpec((rows, depth), lambda t: (0, 0)),
            pl.BlockSpec((depth, tile), lambda t: (0, t + offset)),
            WHOLE,
            ANYWHERE,
        ],
        out_specs=[
            pl.BlockSpec((1, size, LANES), lambda t: (t, 0, 0)),
            pl.BlockSpec((1, blocks, rows // 2, LANES), lambda t: (t, 0, 0, 0)),
        ],
        out_shape=[
            jax.ShapeDtypeStruct((tiles, size, LANES), jnp.int16),
            pltpu.HBM((tiles, blocks, rows // 2, LANES), jnp.float32),
        ],
        compiler_params=params(26),
        cost_estimate=cost(rows, depth, width),
        name="own_z_part",
    )(in_hbm(lam_rows), in_hbm(panel), recv, after)


def own_x_kernel(lam_ref, panel_ref, recv_ref, _, send_ref):
    i_dev = lam_ref.shape[0] // 64
    total = own_sum(lam_ref, panel_ref, recv_ref)
    blocks = total.shape[1] // LANES
    size = 2 * i_dev * 8
    for x in range(4):
        code, level = encode(jnp.concatenate([target_rows(total, x, z, i_dev) for z in range(2)], axis=0))
        for block in range(blocks):
            send_ref[x, 0, block * size : (block + 1) * size, :] = lane_block(code, block)
        send_ref[x, 0, blocks * size :, :] = level_rows(level)


def own_x_part(lam_rows, panel, recv, first, width, tile, after):
    rows, depth = lam_rows.shape
    tiles, offset = width // tile, first // tile
    blocks = tile // LANES
    size = blocks * (rows // 4) + SCALE_ROWS
    return pl.pallas_call(
        own_x_kernel,
        grid=(tiles,),
        in_specs=[
            WHOLE,
            pl.BlockSpec((depth, tile), lambda t: (0, t + offset)),
            WHOLE,
            ANYWHERE,
        ],
        out_specs=pl.BlockSpec((4, 1, size, LANES), lambda t: (0, t, 0, 0)),
        out_shape=jax.ShapeDtypeStruct((4, tiles, size, LANES), jnp.int16),
        compiler_params=params(26),
        cost_estimate=cost(rows, depth, width),
        name="own_x_part",
    )(in_vmem(lam_rows), in_hbm(panel), recv, after)


def merge_z_kernel(keep_ref, recv_ref, _, send_ref):
    blocks, rows = keep_ref.shape[1:3]
    owner = rows // 4
    tile = pl.program_id(0)
    steps = read_steps(recv_ref[tile, blocks * rows :, :])
    totals = []
    for x in range(4):
        for block in range(blocks):
            part = slice(block * rows + x * owner, block * rows + (x + 1) * owner)
            got = decode(recv_ref[tile, part, :], steps[block : block + 1, :])
            totals.append(keep_ref[0, block, x * owner : (x + 1) * owner, :] + got)
    code, level = encode(jnp.concatenate(totals, axis=1))
    for x in range(4):
        for block in range(blocks):
            send_ref[x, 0, block * owner : (block + 1) * owner, :] = lane_block(code, x * blocks + block)
        mine = slice(x * blocks * LANES, (x + 1) * blocks * LANES)
        send_ref[x, 0, blocks * owner :, :] = level_rows(level[:, mine])


def merge_z(keep, recv, after):
    tiles, blocks, rows, _ = keep.shape
    size = blocks * (rows // 4) + SCALE_ROWS
    return pl.pallas_call(
        merge_z_kernel,
        grid=(tiles,),
        in_specs=[
            pl.BlockSpec((1,) + keep.shape[1:], lambda t: (t, 0, 0, 0)),
            WHOLE,
            ANYWHERE,
        ],
        out_specs=pl.BlockSpec((4, 1, size, LANES), lambda t: (0, t, 0, 0)),
        out_shape=jax.ShapeDtypeStruct((4, tiles, size, LANES), jnp.int16),
        compiler_params=params(10),
        cost_estimate=cost(0, 0, 0, 6 * keep.size + 2 * recv.size),
        name="merge_z",
    )(in_hbm(keep), recv, after)


def merge_x_kernel(recv_ref, _, send_ref, keep_ref):
    sources = recv_ref.shape[0]
    tile = pl.program_id(0)
    blocks, owner = keep_ref.shape[1:3]
    rows = 2 * owner
    here = lax.axis_index("z_hi")
    steps = [read_steps(recv_ref[s, tile, blocks * rows :, :]) for s in range(sources)]
    sends = []
    for block in range(blocks):
        part = slice(block * rows, (block + 1) * rows)
        total = sum(decode(recv_ref[s, tile, part, :], steps[s][block : block + 1, :]) for s in range(sources))
        low, high = total[:owner, :], total[owner:, :]
        keep_ref[0, block] = jnp.where(here == 0, low, high)
        sends.append(jnp.where(here == 0, high, low))
    code, level = encode(jnp.concatenate(sends, axis=1))
    for block in range(blocks):
        send_ref[0, block * owner : (block + 1) * owner, :] = lane_block(code, block)
    send_ref[0, blocks * owner :, :] = level_rows(level)


def merge_x(recv, blocks, after):
    sources, tiles, size, _ = recv.shape
    owner = (size - SCALE_ROWS) // blocks // 2
    return pl.pallas_call(
        merge_x_kernel,
        grid=(tiles,),
        in_specs=[
            WHOLE,
            ANYWHERE,
        ],
        out_specs=[
            pl.BlockSpec((1, blocks * owner + SCALE_ROWS, LANES), lambda t: (t, 0, 0)),
            pl.BlockSpec((1, blocks, owner, LANES), lambda t: (t, 0, 0, 0)),
        ],
        out_shape=[
            pltpu.HBM((tiles, blocks * owner + SCALE_ROWS, LANES), jnp.int16),
            pltpu.HBM((tiles, blocks, owner, LANES), jnp.float32),
        ],
        compiler_params=params(10),
        cost_estimate=cost(0, 0, 0, 2 * recv.size),
        name="merge_x",
    )(recv, after)


def finish_kernel(*refs):
    cycle_ref, out_ref = refs[-2:]
    refs = refs[:-2]
    rows = JW // 16 * 8
    i_dev = rows // 8
    blocks = []
    for kind, _, tile_a in CHUNKS:
        count = tile_a * HALVES
        if kind == "z":
            recv_ref, refs = refs[0], refs[1:]
            sources, tiles = recv_ref.shape[:2]
            for tile in range(tiles):
                levels = [read_steps(recv_ref[s, tile, count * rows :, :]) for s in range(sources)]

                def summed(block, ref=recv_ref, tile=tile, levels=levels):
                    part = slice(block * rows, (block + 1) * rows)
                    return sum(
                        decode(ref[s, tile, part, :], levels[s][block : block + 1, :]) for s in range(len(levels))
                    )

                blocks += [functools.partial(summed, block) for block in range(count)]
        else:
            (keep_ref, recv_ref), refs = refs[:2], refs[2:]
            for tile in range(recv_ref.shape[0]):
                levels = read_steps(recv_ref[tile, count * rows :, :])

                def kept(block, keep=keep_ref, ref=recv_ref, tile=tile, levels=levels):
                    part = slice(block * rows, (block + 1) * rows)
                    return keep[tile, block] + decode(ref[tile, part, :], levels[block : block + 1, :])

                blocks += [functools.partial(kept, block) for block in range(count)]

    for group in range(AW // 8):

        @pl.when(pl.program_id(0) == group)
        def _group(group=group):
            for half in range(HALVES):
                totals = [blocks[(group * 8 + a) * HALVES + half]() for a in range(8)]
                for i in range(i_dev):
                    stack = jnp.stack([total[i * 8 : (i + 1) * 8, :] for total in totals], axis=0)
                    turned = jnp.swapaxes(stack, 0, 1)
                    for jj in range(8):
                        lanes = pl.ds(jj * BW + half * LANES, LANES)
                        out_ref[i, 0, :, lanes] = turned[jj] + cycle_ref[i, 0, :, lanes]


def finish(parts, cycle):
    rows, columns = cycle.shape
    shape = (rows // AW, AW // 8, 8, columns)
    block = pl.BlockSpec((shape[0], 1, 8, columns), lambda t: (0, t, 0, 0))
    out = pl.pallas_call(
        finish_kernel,
        grid=(AW // 8,),
        in_specs=[WHOLE] * len(parts) + [block],
        out_specs=block,
        out_shape=pltpu.HBM(shape, jnp.float32),
        compiler_params=params(12),
        cost_estimate=cost(0, 0, 0, 16 * cycle.size),
        name="finish",
    )(*[in_hbm(part) if part.dtype == jnp.float32 else in_vmem(part) for part in parts], cycle.reshape(shape))
    return out.reshape(rows, columns)


def one_hot_places(virt):
    start = jnp.zeros(virt.shape, jnp.int32)
    for label in range(8):
        below = jnp.sum((virt < label).astype(jnp.int32), axis=1, keepdims=True)
        start = jnp.where(virt == label, below, start)
    place = lax.broadcasted_iota(jnp.int32, virt.shape, 1) - start
    return lax.broadcasted_iota(jnp.int32, (SEGMENT, BW), 0) == place


def spread_matrix(virt):
    hot = one_hot_places(virt).astype(jnp.float32)
    none = jnp.zeros_like(hot)
    group = LANES // SEGMENT
    rows = [jnp.concatenate([hot if a == b else none for b in range(group)], axis=1) for a in range(group)]
    return jnp.concatenate(rows, axis=0).astype(jnp.bfloat16)


def row_labels(occ, virt, first, rows):
    row = lax.broadcasted_iota(jnp.int32, (rows, 1), 0)
    k = first + row // PAN
    lane = lax.broadcasted_iota(jnp.int32, (rows, occ.shape[1]), 1)
    k_label = jnp.sum(jnp.where(lane == k, occ, 0), axis=1, keepdims=True)
    lane = lax.broadcasted_iota(jnp.int32, (rows, LANES), 1)
    c_label = jnp.sum(jnp.where(lane == row % PAN, virt[:, :LANES], 0), axis=1, keepdims=True)
    return k_label ^ c_label


def pack_kernel(occ_s_ref, occ_ref, virt_ref, cycle_ref, packed_ref, jb_ref):
    rows, columns = cycle_ref.shape
    virt = virt_ref[...]
    mine = row_labels(occ_ref[...], virt, lax.axis_index(OCC) * (rows // PAN), rows)
    spread = spread_matrix(virt)
    width = spread.shape[1]
    for step in range(columns // width):
        lanes = slice(step * width, (step + 1) * width)
        first = (lax.axis_index(VIR) * (columns // width) + step) * (width // BW)
        jb = jnp.concatenate([virt ^ occ_s_ref[first + jj] for jj in range(width // BW)], axis=1)
        jb_ref[:, lanes] = jb
        masked = jnp.where(mine == jb, cycle_ref[:, lanes].astype(jnp.float32), 0.0).astype(jnp.bfloat16)
        packed_ref[:, step * LANES : (step + 1) * LANES] = lax.dot_general(
            masked, spread, (((1,), (1,)), ((), ())), preferred_element_type=jnp.float32
        ).astype(jnp.bfloat16)


def pack(occ_irrep, virt_irrep, cycle_int):
    rows, columns = cycle_int.shape
    width = columns * SEGMENT // BW
    return pl.pallas_call(
        pack_kernel,
        in_specs=[SCALARS, WHOLE, WHOLE, WHOLE],
        out_shape=[
            jax.ShapeDtypeStruct((rows, width), jnp.bfloat16),
            jax.ShapeDtypeStruct((1, columns), jnp.int32),
        ],
        compiler_params=params(12),
        cost_estimate=cost(rows, LANES, columns),
        name="pack",
    )(occ_irrep, occ_irrep[None, :], virt_irrep[None, :], in_hbm(cycle_int))


def lane_labels(occ_s, virt_s, depth):
    lane = lax.broadcasted_iota(jnp.int32, (1, LANES), 1)
    c_label = jnp.zeros((1, LANES), jnp.int32)
    for c in range(PAN):
        c_label = jnp.where(lane % PAN == c, virt_s[c], c_label)
    pieces = []
    per_row = LANES // PAN
    for row in range(depth // LANES):
        k_label = jnp.zeros((1, LANES), jnp.int32)
        for m in range(per_row):
            k_label = jnp.where(lane // PAN == m, occ_s[row * per_row + m], k_label)
        pieces.append(k_label ^ c_label)
    return jnp.concatenate(pieces, axis=1)


def cycle_kernel(occ_s_ref, virt_s_ref, virt_ref, jb_ref, amp_ref, packed_ref, _, out_ref, split_ref):
    rows, depth = amp_ref.shape
    width = LANES // SEGMENT * BW

    @pl.when(pl.program_id(0) == 0)
    def _split():
        label = lane_labels(occ_s_ref, virt_s_ref, depth)
        amp = amp_ref[...].astype(jnp.float32)
        for g in range(8):
            split_ref[g * rows : (g + 1) * rows, :] = jnp.where(label == g, amp, 0.0).astype(jnp.bfloat16)

    parts = jnp.dot(split_ref[...], packed_ref[...], preferred_element_type=jnp.float32)
    spread = spread_matrix(virt_ref[...]).astype(jnp.float32)
    for pair in range(packed_ref.shape[1] // LANES):
        lanes = slice(pair * LANES, (pair + 1) * LANES)
        wide = jnp.concatenate([parts[g * rows : (g + 1) * rows, lanes] for g in range(8)], axis=1)
        high = wide.astype(jnp.bfloat16)
        low = (wide - high.astype(jnp.float32)).astype(jnp.bfloat16)
        jb = jb_ref[:, pair * width : (pair + 1) * width]
        choose = jnp.concatenate([jnp.where(jb == g, spread, 0.0).astype(jnp.bfloat16) for g in range(8)], axis=0)
        both = jnp.dot(jnp.concatenate([high, low], axis=0), choose, preferred_element_type=jnp.float32)
        out_ref[:, pair * width : (pair + 1) * width] = both[:rows, :] + both[rows:, :]


def cycle_term(occ_irrep, virt_irrep, jb_irrep, amp, packed, after):
    rows, depth = amp.shape
    steps = 2
    columns = jb_irrep.shape[1]
    return pl.pallas_call(
        cycle_kernel,
        grid=(steps,),
        in_specs=[
            SCALARS,
            SCALARS,
            WHOLE,
            pl.BlockSpec((1, columns // steps), lambda t: (0, t)),
            pl.BlockSpec((rows, depth), lambda t: (0, 0)),
            pl.BlockSpec((depth, packed.shape[1] // steps), lambda t: (0, t)),
            ANYWHERE,
        ],
        out_specs=pl.BlockSpec((rows, columns // steps), lambda t: (0, t)),
        out_shape=jax.ShapeDtypeStruct((rows, columns), jnp.float32),
        scratch_shapes=[pltpu.VMEM((8 * rows, depth), jnp.bfloat16)],
        compiler_params=params(28),
        cost_estimate=cost(2 * rows, depth, columns),
        name="cycle_term",
    )(in_hbm(occ_irrep), in_hbm(virt_irrep), virt_irrep[None, :], jb_irrep, in_hbm(amp), in_hbm(packed), after)


def swap(value, axis):
    return lax.ppermute(value, axis, [(0, 1), (1, 0)])


def exchange(value):
    return lax.all_to_all(value, "x", 0, 0)


def dense_cycle(amp, cycle_int, occ_irrep, virt_irrep, j_first, j_width):
    gathered = lax.all_gather(cycle_int, OCC, axis=0, tiled=True)
    kc_irrep = (occ_irrep[:, None] ^ virt_irrep[None, :PAN]).reshape(-1)
    jb_irrep = lax.dynamic_slice_in_dim(occ_irrep, j_first, j_width, 0)[:, None] ^ virt_irrep[None, :]
    allowed = kc_irrep[:, None] == jb_irrep.reshape(1, -1)
    masked = jnp.where(allowed, gathered, jnp.zeros((), gathered.dtype))
    return jnp.dot(amp, masked, preferred_element_type=jnp.float32)


def per_device(lam, ladder_int, cycle_amp, cycle_int, occ_irrep, virt_irrep):
    j_width = JW // lax.axis_size(VIR)
    j_first = lax.axis_index(VIR) * j_width
    fits = jnp.all(virt_irrep[SEGMENT:] != virt_irrep[:-SEGMENT])
    last, jb_irrep = pack(occ_irrep, virt_irrep, cycle_int)
    gathered = lax.all_gather(last, OCC, axis=0, tiled=True)

    kinds = [kind for kind, _, _ in CHUNKS]
    widths = [a * BW for _, a, _ in CHUNKS]
    tiles = [a * BW for _, _, a in CHUNKS]
    firsts = [sum(widths[:n]) for n in range(len(CHUNKS))]
    lam_rows = {}
    core_got, sent, kept, second = {}, {}, {}, {}

    def partner(n, last):
        if not lam_rows:
            last, lam_rows["own"], lam_rows["other"] = first_partner_part(
                lam, ladder_int, firsts[n], widths[n], tiles[n], last
            )
        else:
            last = partner_part(lam_rows["other"], ladder_int, firsts[n], widths[n], tiles[n], last)
        core_got[n] = swap(last, "core")
        return last

    def own(n, last):
        args = (lam_rows["own"], ladder_int, core_got[n], firsts[n], widths[n], tiles[n], last)
        if kinds[n] == "z":
            last, kept[n] = own_z_part(*args)
            sent[n] = swap(last, "z_hi")
        else:
            last = own_x_part(*args)
            sent[n] = exchange(last)
        return last

    def merge(n, last):
        if kinds[n] == "z":
            last = merge_z(kept[n], sent[n], last)
            second[n] = [exchange(last)]
        else:
            last, keep = merge_x(sent[n], tiles[n] // LANES, last)
            second[n] = [keep, swap(last, "z_hi")]
        return last

    for step in ORDER:
        if step == "C":
            cycle = lax.cond(
                fits,
                lambda gathered, jb, amp, own, occ, virt, last: cycle_term(occ, virt, jb, amp, gathered, last),
                lambda gathered, jb, amp, own, occ, virt, last: dense_cycle(amp, own, occ, virt, j_first, j_width),
                *(gathered, jb_irrep, cycle_amp, cycle_int, occ_irrep, virt_irrep, last),
            )
            last = cycle
        else:
            last = {"P": partner, "O": own, "M": merge}[step[0]](int(step[1]), last)
    return finish([part for n in range(len(CHUNKS)) for part in second[n]], cycle)


def solution(mesh):
    fine = Mesh(mesh.devices.reshape(2, 4, 4, 2, 2), ("z_lo", "y", "x", "z_hi", "core"))
    return jax.shard_map(
        per_device,
        mesh=fine,
        in_specs=(P(OCC, VIR), P(VIR, None), P(OCC, None), P(OCC, VIR), P(), P()),
        out_specs=P(OCC, VIR),
        check_vma=False,
    )
```

time: 312 us -> 106 us (0.34)
  waiting for transfers between devices: 244 us -> 18 us
  Pallas kernels: 0 us -> 53.4 us
  matrix products: 30.4 us -> 0 us
  local copies, waits for them, and re-layouts: 21.8 us -> 3.9 us
  starting transfers between devices: 0.05 us -> 15.4 us
    reduce_scatter x1 -> x0, waiting for transfers between devices: 243 us -> none  [per_device(): lax.psum_scatter(jnp.einsum('ijk,kn->jin', lam_blocks, ladder_int, prefer...]
    pallas_call x0 -> x9, Pallas kernels: none -> 53.4 us  [the longest x1 10.5 us: cycle_term(): pl.pallas_call(cycle_kernel, grid=(steps,), in_specs=[SCALARS, SCALARS, W...]
    dot_general x2 -> x0, matrix products: 30.4 us -> none  [the longest x1 21.2 us: per_device(): jnp.einsum('ijk,kn->jin', lam_blocks, ladder_int, preferred_element_type=...]
    transpose x1 -> x0, local copies, waits for them, and re-layouts: 17.7 us -> none  [per_device(): jnp.einsum('ijk,kn->jin', lam_blocks, ladder_int, preferred_element_type=...]
    ppermute x0 -> x4, waiting for transfers between devices: none -> 9.67 us  [swap(): return lax.ppermute(value, axis, [(0, 1), (1, 0)])]
    all_to_all x0 -> x2, starting transfers between devices: none -> 8.64 us  [exchange(): return lax.all_to_all(value, 'x', 0, 0)]
    ppermute x0 -> x4, starting transfers between devices: none -> 6.77 us  [swap(): return lax.ppermute(value, axis, [(0, 1), (1, 0)])]
    all_gather x1, waiting for transfers between devices: 0.03 us -> 4.95 us  [per_device(): gathered = lax.all_gather(last, OCC, axis=0, tiled=True)]
  transfers between devices with their start and end apart: 2 -> 7, of which waited for: 1 -> 5; matrix products, arithmetic and copies ran while one was open for 1% -> 3% of each run, Pallas kernels for 0% -> 42%
where the time goes in v2:
time: 106 us; the launch traced here: 105 us
  Pallas kernels  53.4 us (50%)
  waiting for transfers between devices  18 us (17%)
  starting transfers between devices  15.4 us (15%)
  between operations  14 us (13%)
  local copies, waits for them, and re-layouts  3.9 us (4%)
    pallas_call x1, Pallas kernels, cycle_term(): pl.pallas_call(cycle_kernel, grid=(steps,), in_specs=[SCALARS, SCALARS, W...  10.5 us
    pallas_call x1, Pallas kernels, first_partner_part(): pl.pallas_call(first_partner_kernel, grid=(tiles,), in_specs=[pl.BlockSpe...  10.1 us
    ppermute x4, waiting for transfers between devices, swap(): return lax.ppermute(value, axis, [(0, 1), (1, 0)])  9.67 us
    pallas_call x1, Pallas kernels, own_x_part(): pl.pallas_call(own_x_kernel, grid=(tiles,), in_specs=[WHOLE, pl.BlockSpec...  9.35 us
    all_to_all x2, starting transfers between devices, exchange(): return lax.all_to_all(value, 'x', 0, 0)  8.64 us
    pallas_call x1, Pallas kernels, own_z_part(): pl.pallas_call(own_z_kernel, grid=(tiles,), in_specs=[pl.BlockSpec((rows,...  7.6 us
    ppermute x4, starting transfers between devices, swap(): return lax.ppermute(value, axis, [(0, 1), (1, 0)])  6.77 us
    pallas_call x1, Pallas kernels, partner_part(): pl.pallas_call(partner_kernel, grid=(tiles,), in_specs=[WHOLE, pl.BlockSp...  5.22 us
  transfers between devices with their start and end apart: 7, of which 5 were waited for; matrix products, arithmetic and copies ran while one was open for 3% of the time, Pallas kernels for 42%

profile of v2, /device:TPU:0, one launch (start us, length us, event | category | flops | bytes accessed | tf_op | source)
XLA Modules:
  0.0 105.5 jit_solution(15675772081914427301)
XLA Ops:
  6.5 0.0 all-gather.5.cloned.1.call-start
  6.5 3.0 %pack.1 = (bf16[400,512]{1,0:T(8,128)(2,1)}, s32[1,2048]{1,0:T(1,128)}) custom-call(s32[200]{0:T(256)} %occ_s_ref.1, s32[1,200]{1,0:T(1,128)} %bitcast.14, s32[1,256]{1,0:T(1,128)} %bitcast.12, bf16[400,2048]{1,0:T(8,128)(2,1)} %cycle_ref.1), custom_call_target="tpu_custom_call" | custom-call | flops 26214400 | bytes 78337 | tf_op jit(solution)/shard_map/pack/pallas_call | solution.py:447
  9.5 0.0 all-gather.5.cloned.1.call-update
  9.6 0.0 copy-start
  9.6 10.1 %partner_part.2 = (s16[2,5136,128]{2,1,0:T(8,128)(2,1)S(1)}, bf16[512,1792]{1,0:T(8,128)(2,1)S(1)}, bf16[512,1792]{1,0:T(8,128)(2,1)S(1)}) custom-call(bf16[1024,1792]{1,0:T(8,128)(2,1)} %lam_ref.1, bf16[1792,4096]{1,0:T(8,128)(2,1)} %panel_ref.7, bf16[400,512]{1,0:T(8,128)(2,1)} %get-tuple-element.51._), custom_call_target="tpu_custom_call" | custom-call | flops 587202560 | bytes 1376257 | tf_op jit(solution)/shard_map/partner_part/pallas_call | solution.py:111
  19.7 0.0 copy-start.1
  19.7 0.1 collective-permute-start
  19.8 0.0 copy-done
  19.8 5.2 %partner_part.3._ = s16[3,2064,128]{2,1,0:T(8,128)(2,1)} custom-call(bf16[512,1792]{1,0:T(8,128)(2,1)S(1)} %get-tuple-element.54.lam_ref, bf16[1792,4096]{1,0:T(8,128)(2,1)S(1)} %copy-done, s16[2,5136,128]{2,1,0:T(8,128)(2,1)S(1)} %get-tuple-element.53._), custom_call_target="tpu_custom_call" | custom-call | flops 352321536 | bytes 917505 | tf_op jit(solution)/shard_map/partner_part/pallas_call | solution.py:143
  25.0 0.5 collective-permute-start.1
  25.5 0.0 collective-permute-done.recv_ref
  25.5 0.0 copy-done.1
  25.5 9.3 %own_x_part.1._ = s16[4,2,1296,128]{3,2,1,0:T(8,128)(2,1)} custom-call(bf16[512,1792]{1,0:T(8,128)(2,1)S(1)} %get-tuple-element.52.lam_ref, bf16[1792,4096]{1,0:T(8,128)(2,1)} %panel_ref.7, s16[2,5136,128]{2,1,0:T(8,128)(2,1)S(1)} %collective-permute-done.recv_ref, s16[3,2064,128]{2,1,0:T(8,128)(2,1)} %partner_part.3._), custom_call_target="tpu_custom_call" | custom-call | flops 587202560 | bytes 1376257 | tf_op jit(solution)/shard_map/own_x_part/pallas_call | solution.py:238
  34.8 4.4 %all-to-all-start = ((s16[4,2,1296,128]{3,2,1,0:T(8,128)(2,1)}), s16[4,2,1296,128]{3,2,1,0:T(8,128)(2,1)S(1)}, u32[]{:S(2)}, u32[]{:S(2)}) async-start(s16[4,2,1296,128]{3,2,1,0:T(8,128)(2,1)} %own_x_part.1._), calls=%async_computation | async-start | bytes 5308416 | tf_op jit(solution)/shard_map/all_to_all | solution.py:529
  39.2 0.0 copy-start.4
  39.2 0.0 collective-permute-done.1.recv_ref
  39.2 7.6 %own_z_part.1 = (s16[3,1040,128]{2,1,0:T(8,128)(2,1)}, f32[3,4,256,128]{3,2,1,0:T(8,128)}) custom-call(bf16[512,1792]{1,0:T(8,128)(2,1)} %copy-done.1, bf16[1792,4096]{1,0:T(8,128)(2,1)} %panel_ref.7, s16[3,2064,128]{2,1,0:T(8,128)(2,1)} %collective-permute-done.1.recv_ref, s16[4,2,1296,128]{3,2,1,0:T(8,128)(2,1)} %own_x_part.1._), custom_call_target="tpu_custom_call" | custom-call | flops 352321536 | bytes 917505 | tf_op jit(solution)/shard_map/own_z_part/pallas_call | solution.py:198
  46.8 3.9 %collective-permute-start.3 = (s16[3,1040,128]{2,1,0:T(8,128)(2,1)}, s16[3,1040,128]{2,1,0:T(8,128)(2,1)S(1)}, u32[]{:S(2)}, u32[]{:S(2)}) collective-permute-start(s16[3,1040,128]{2,1,0:T(8,128)(2,1)} %get-tuple-element.56), channel_id=1, source_target_pairs={{0,2},{2,0},{1,3},{3,1},{4,6},{6,4},{5,7},{7,5},{8,10},{10,8},{9,1... | collective-permute-start | bytes 2396168 | tf_op jit(solution)/shard_map/ppermute | solution.py:525
  50.7 0.0 copy-done.4
  50.7 0.7 compare_reduce_fusion
  52.0 4.9 %all-gather.5.cloned.1.call-done = bf16[3200,512]{1,0:T(8,128)(2,1)} async-done(((bf16[400,512]{1,0:T(8,128)(2,1)}), bf16[3200,512]{1,0:T(8,128)(2,1)}) %all-gather.5.cloned.1.call-update) | async-done | bytes 3276816 | tf_op jit(solution)/shard_map/all_gather | solution.py:546
  56.9 13.4 %conditional.1 = (f32[128,2048]{1,0:T(8,128)}, f32[8,2,8,2048]{3,2,1,0:T(8,128)}) conditional(s32[]{:T(128)} %convert_element_type.3, (s32[200]{0:T(256)}, s32[256]{0:T(256)S(1)}, s32[]{:T(128)}, bf16[400,2048]{1,0:T(8,128)(2,1)}, bf16[128,3200]{1,0:T(8,128)(2,1)}, /*index=5*/(), s32[]{:T(128)}, s32[]{:T(128)}, (), ()) %tuple.32, (s32[256]{0:T(256)S(1)}, ...), branch_computations={%region_1.2_spmd, %region_2.3_spmd} | conditional | flops 1690834048 | bytes 61395160 | solution.py:586
  56.9 0.0 copy-start.5
  56.9 0.6 copy-done.5
  57.5 10.5 %cycle_term.1 = f32[128,2048]{1,0:T(8,128)} custom-call(s32[200]{0:T(256)} %get-tuple-element.34.occ_s_ref, s32[256]{0:T(256)} %copy-done.5, s32[1,256]{1,0:T(1,128)} %bitcast.13, s32[1,2048]{1,0:T(1,128)} %get-tuple-element.36.jb_ref, bf16[128,3200]{1,0:T(8,128)(2,1)} %get-tuple-element.37.amp_ref, bf16[3200,512]{1,0:T(8,128)(2,1)} %get-tuple-element.38.packed_ref, ...), custom_call_target="tpu_custom_call" | custom-call | flops 419430400 | bytes 1843201 | tf_op jit(solution)/shard_map/cond/branch_1_fun/cycle_term/pallas_call | solution.py:503
  68.0 2.3 %copy.11 = f32[8,2,8,2048]{3,2,1,0:T(8,128)} copy(f32[8,2,8,2048]{3,2,1,0:T(8,128)} %bitcast.3) | data formatting | bytes 2097152 | tf_op jit(solution)/shard_map/cond
  70.3 1.5 %all-to-all-done.recv_ref = s16[4,2,1296,128]{3,2,1,0:T(8,128)(2,1)S(1)} async-done(((s16[4,2,1296,128]{3,2,1,0:T(8,128)(2,1)}), s16[4,2,1296,128]{3,2,1,0:T(8,128)(2,1)S(1)}, u32[]{:S(2)}, u32[]{:S(2)}) %all-to-all-start) | async-done | bytes 2654240 | tf_op jit(solution)/shard_map/all_to_all | solution.py:529
  71.7 1.7 %merge_x.1 = (s16[2,656,128]{2,1,0:T(8,128)(2,1)}, f32[2,10,64,128]{3,2,1,0:T(8,128)}) custom-call(s16[4,2,1296,128]{3,2,1,0:T(8,128)(2,1)S(1)} %all-to-all-done.recv_ref, f32[128,2048]{1,0:T(8,128)} %get-tuple-element.57._), custom_call_target="tpu_custom_call" | custom-call | bytes 331777 | tf_op jit(solution)/shard_map/merge_x/pallas_call | solution.py:316
  73.4 0.9 collective-permute-done.3.recv_ref
  74.3 0.0 copy-start.2
  74.3 1.0 copy-done.2
  75.3 0.0 copy-start.3
  75.3 3.4 %merge_z.1 = s16[4,3,272,128]{3,2,1,0:T(8,128)(2,1)} custom-call(f32[3,4,256,128]{3,2,1,0:T(8,128)} %get-tuple-element.60.keep_ref, s16[3,1040,128]{2,1,0:T(8,128)(2,1)S(1)} %collective-permute-done.3.recv_ref, s16[2,656,128]{2,1,0:T(8,128)(2,1)S(1)} %copy-done.2), custom_call_target="tpu_custom_call" | custom-call | bytes 394753 | tf_op jit(solution)/shard_map/merge_z/pallas_call | solution.py:277
  78.8 4.2 %all-to-all-start.1 = ((s16[4,3,272,128]{3,2,1,0:T(8,128)(2,1)}), s16[4,3,272,128]{3,2,1,0:T(8,128)(2,1)S(1)}, u32[]{:S(2)}, u32[]{:S(2)}) async-start(s16[4,3,272,128]{3,2,1,0:T(8,128)(2,1)} %merge_z.1), calls=%async_computation.1 | async-start | bytes 1671168 | tf_op jit(solution)/shard_map/all_to_all | solution.py:529
  83.0 0.0 copy-done.3
  83.0 2.3 %collective-permute-start.2 = (s16[2,656,128]{2,1,0:T(8,128)(2,1)S(1)}, s16[2,656,128]{2,1,0:T(8,128)(2,1)S(1)}, u32[]{:S(2)}, u32[]{:S(2)}) collective-permute-start(s16[2,656,128]{2,1,0:T(8,128)(2,1)S(1)} %copy-done.3), channel_id=1, source_target_pairs={{0,2},{2,0},{1,3},{3,1},{4,6},{6,4},{5,7},{7,5},{8,10},{10,8},{9,1... | collective-permute-start | bytes 1007624 | tf_op jit(solution)/shard_map/ppermute | solution.py:525
  85.3 8.7 %collective-permute-done.2.refs_1_ = s16[2,656,128]{2,1,0:T(8,128)(2,1)S(1)} collective-permute-done((s16[2,656,128]{2,1,0:T(8,128)(2,1)S(1)}, s16[2,656,128]{2,1,0:T(8,128)(2,1)S(1)}, u32[]{:S(2)}, u32[]{:S(2)}) %collective-permute-start.2) | collective-permute-done | bytes 335904 | tf_op jit(solution)/shard_map/ppermute | solution.py:525
  94.0 2.0 %all-to-all-done.1.refs_2_ = s16[4,3,272,128]{3,2,1,0:T(8,128)(2,1)S(1)} async-done(((s16[4,3,272,128]{3,2,1,0:T(8,128)(2,1)}), s16[4,3,272,128]{3,2,1,0:T(8,128)(2,1)S(1)}, u32[]{:S(2)}, u32[]{:S(2)}) %all-to-all-start.1) | async-done | bytes 835616 | tf_op jit(solution)/shard_map/all_to_all | solution.py:529
  96.0 2.6 %finish.1 = f32[8,2,8,2048]{3,2,1,0:T(8,128)} custom-call(f32[2,10,64,128]{3,2,1,0:T(8,128)} %get-tuple-element.58.refs_0_, s16[2,656,128]{2,1,0:T(8,128)(2,1)S(1)} %collective-permute-done.2.refs_1_, s16[4,3,272,128]{3,2,1,0:T(8,128)(2,1)S(1)} %all-to-all-done.1.refs_2_, f32[8,2,8,2048]{3,2,1,0:T(8,128)} %get-tuple-element.61.refs_3_), custom_call_target="tpu_custom_call" | custom-call | bytes 524289 | tf_op jit(solution)/shard_map/finish/pallas_call | solution.py:387
Async XLA Ops:
  6.5 50.4 %all-gather.5.cloned.1.call-start = ((), (), s32[]{:S(2)}) async-start(), calls=%async_computation.3 | async-start | bytes 3686400 | tf_op jit(solution)/shard_map/all_gather | solution.py:546
  9.6 10.2 %copy-start = (bf16[1792,4096]{1,0:T(8,128)(2,1)S(1)}, bf16[1792,4096]{1,0:T(8,128)(2,1)}, u32[]{:S(2)}) copy-start(bf16[1792,4096]{1,0:T(8,128)(2,1)} %panel_ref.7) | copy-start | bytes 44040196
  19.7 5.8 %copy-start.1 = (bf16[512,1792]{1,0:T(8,128)(2,1)}, bf16[512,1792]{1,0:T(8,128)(2,1)S(1)}, u32[]{:S(2)}) copy-start(bf16[512,1792]{1,0:T(8,128)(2,1)S(1)} %get-tuple-element.52.lam_ref) | copy-start | bytes 5505028
  19.7 5.8 %collective-permute-start = (s16[2,5136,128]{2,1,0:T(8,128)(2,1)S(1)}, s16[2,5136,128]{2,1,0:T(8,128)(2,1)S(1)}, u32[]{:S(2)}, u32[]{:S(2)}) collective-permute-start(s16[2,5136,128]{2,1,0:T(8,128)(2,1)S(1)} %get-tuple-element.53._), channel_id=1, source_target_pairs={{0,1},{1,0},{2,3},{3,2},{4,5},{5,4},{6,7},{7,6},{8,9},{9,8},{10,11... | collective-permute-start | bytes 7888904 | tf_op jit(solution)/shard_map/ppermute | solution.py:525
  25.0 14.2 %collective-permute-start.1 = (s16[3,2064,128]{2,1,0:T(8,128)(2,1)}, s16[3,2064,128]{2,1,0:T(8,128)(2,1)}, u32[]{:S(2)}, u32[]{:S(2)}) collective-permute-start(s16[3,2064,128]{2,1,0:T(8,128)(2,1)} %partner_part.3._), channel_id=1, source_target_pairs={{0,1},{1,0},{2,3},{3,2},{4,5},{5,4},{6,7},{7,6},{8,9},{9,8},{10,11... | collective-permute-start | bytes 4755464 | tf_op jit(solution)/shard_map/ppermute | solution.py:525
  34.8 36.9 %all-to-all-start = ((s16[4,2,1296,128]{3,2,1,0:T(8,128)(2,1)}), s16[4,2,1296,128]{3,2,1,0:T(8,128)(2,1)S(1)}, u32[]{:S(2)}, u32[]{:S(2)}) async-start(s16[4,2,1296,128]{3,2,1,0:T(8,128)(2,1)} %own_x_part.1._), calls=%async_computation | async-start | bytes 5308416 | tf_op jit(solution)/shard_map/all_to_all | solution.py:529
  39.2 11.5 %copy-start.4 = (s32[256]{0:T(256)S(1)}, s32[256]{0:T(256)}, u32[]{:S(2)}) copy-start(s32[256]{0:T(256)} %param.13) | copy-start | bytes 3076
  46.8 27.5 %collective-permute-start.3 = (s16[3,1040,128]{2,1,0:T(8,128)(2,1)}, s16[3,1040,128]{2,1,0:T(8,128)(2,1)S(1)}, u32[]{:S(2)}, u32[]{:S(2)}) collective-permute-start(s16[3,1040,128]{2,1,0:T(8,128)(2,1)} %get-tuple-element.56), channel_id=1, source_target_pairs={{0,2},{2,0},{1,3},{3,1},{4,6},{6,4},{5,7},{7,5},{8,10},{10,8},{9,1... | collective-permute-start | bytes 2396168 | tf_op jit(solution)/shard_map/ppermute | solution.py:525
  56.9 0.6 copy-start.5
  74.3 1.0 copy-start.2
  75.3 7.7 %copy-start.3 = (s16[2,656,128]{2,1,0:T(8,128)(2,1)S(1)}, s16[2,656,128]{2,1,0:T(8,128)(2,1)}, u32[]{:S(2)}) copy-start(s16[2,656,128]{2,1,0:T(8,128)(2,1)} %get-tuple-element.59._) | copy-start | bytes 1007620
  78.8 17.2 %all-to-all-start.1 = ((s16[4,3,272,128]{3,2,1,0:T(8,128)(2,1)}), s16[4,3,272,128]{3,2,1,0:T(8,128)(2,1)S(1)}, u32[]{:S(2)}, u32[]{:S(2)}) async-start(s16[4,3,272,128]{3,2,1,0:T(8,128)(2,1)} %merge_z.1), calls=%async_computation.1 | async-start | bytes 1671168 | tf_op jit(solution)/shard_map/all_to_all | solution.py:529
  83.0 11.0 %collective-permute-start.2 = (s16[2,656,128]{2,1,0:T(8,128)(2,1)S(1)}, s16[2,656,128]{2,1,0:T(8,128)(2,1)S(1)}, u32[]{:S(2)}, u32[]{:S(2)}) collective-permute-start(s16[2,656,128]{2,1,0:T(8,128)(2,1)S(1)} %copy-done.3), channel_id=1, source_target_pairs={{0,2},{2,0},{1,3},{3,1},{4,6},{6,4},{5,7},{7,5},{8,10},{10,8},{9,1... | collective-permute-start | bytes 1007624 | tf_op jit(solution)/shard_map/ppermute | solution.py:525
Sparse Core Ops, SparseCore 0:
  9.7 47.1 all-gather.4

commit v3 on v2

--- a/solution.py
+++ b/solution.py
@@ -153,7 +153,7 @@
         compiler_params=params(20),
         cost_estimate=cost(rows, depth, width),
         name="partner_part",
-    )(in_vmem(lam_rows), panel, after)
+    )(in_vmem(lam_rows), in_vmem(panel), after)
 
 
 def own_sum(lam_ref, panel_ref, recv_ref):
@@ -249,7 +249,7 @@
         compiler_params=params(26),
         cost_estimate=cost(rows, depth, width),
         name="own_x_part",
-    )(in_vmem(lam_rows), in_hbm(panel), recv, after)
+    )(in_vmem(lam_rows), in_vmem(panel), recv, after)
 
 
 def merge_z_kernel(keep_ref, recv_ref, _, send_ref):
@@ -262,7 +262,7 @@
         for block in range(blocks):
             part = slice(block * rows + x * owner, block * rows + (x + 1) * owner)
             got = decode(recv_ref[tile, part, :], steps[block : block + 1, :])
-            totals.append(keep_ref[0, block, x * owner : (x + 1) * owner, :] + got)
+            totals.append(keep_ref[tile, block, x * owner : (x + 1) * owner, :] + got)
     code, level = encode(jnp.concatenate(totals, axis=1))
     for x in range(4):
         for block in range(blocks):
@@ -278,7 +278,7 @@
         merge_z_kernel,
         grid=(tiles,),
         in_specs=[
-            pl.BlockSpec((1,) + keep.shape[1:], lambda t: (t, 0, 0, 0)),
+            WHOLE,
             WHOLE,
             ANYWHERE,
         ],
@@ -287,7 +287,7 @@
         compiler_params=params(10),
         cost_estimate=cost(0, 0, 0, 6 * keep.size + 2 * recv.size),
         name="merge_z",
-    )(in_hbm(keep), recv, after)
+    )(in_vmem(keep), recv, in_hbm(after))
 
 
 def merge_x_kernel(recv_ref, _, send_ref, keep_ref):
@@ -381,8 +381,8 @@
 
 
 def finish(parts, cycle):
-    rows, columns = cycle.shape
-    shape = (rows // AW, AW // 8, 8, columns)
+    shape = cycle.shape
+    columns = shape[-1]
     block = pl.BlockSpec((shape[0], 1, 8, columns), lambda t: (0, t, 0, 0))
     out = pl.pallas_call(
         finish_kernel,
@@ -393,8 +393,8 @@
         compiler_params=params(12),
         cost_estimate=cost(0, 0, 0, 16 * cycle.size),
         name="finish",
-    )(*[in_hbm(part) if part.dtype == jnp.float32 else in_vmem(part) for part in parts], cycle.reshape(shape))
-    return out.reshape(rows, columns)
+    )(*[in_hbm(part) if part.dtype == jnp.float32 else in_vmem(part) for part in parts], cycle)
+    return out.reshape(-1, columns)
 
 
 def one_hot_places(virt):
@@ -493,13 +493,14 @@
         jb = jb_ref[:, pair * width : (pair + 1) * width]
         choose = jnp.concatenate([jnp.where(jb == g, spread, 0.0).astype(jnp.bfloat16) for g in range(8)], axis=0)
         both = jnp.dot(jnp.concatenate([high, low], axis=0), choose, preferred_element_type=jnp.float32)
-        out_ref[:, pair * width : (pair + 1) * width] = both[:rows, :] + both[rows:, :]
+        out_ref[..., pair * width : (pair + 1) * width] = (both[:rows, :] + both[rows:, :]).reshape(out_ref.shape[:3] + (width,))
 
 
 def cycle_term(occ_irrep, virt_irrep, jb_irrep, amp, packed, after):
     rows, depth = amp.shape
     steps = 2
     columns = jb_irrep.shape[1]
+    shape = (rows // AW, AW // 8, 8, columns)
     return pl.pallas_call(
         cycle_kernel,
         grid=(steps,),
@@ -512,8 +513,8 @@
             pl.BlockSpec((depth, packed.shape[1] // steps), lambda t: (0, t)),
             ANYWHERE,
         ],
-        out_specs=pl.BlockSpec((rows, columns // steps), lambda t: (0, t)),
-        out_shape=jax.ShapeDtypeStruct((rows, columns), jnp.float32),
+        out_specs=pl.BlockSpec(shape[:3] + (columns // steps,), lambda t: (0, 0, 0, t)),
+        out_shape=pltpu.HBM(shape, jnp.float32),
         scratch_shapes=[pltpu.VMEM((8 * rows, depth), jnp.bfloat16)],
         compiler_params=params(28),
         cost_estimate=cost(2 * rows, depth, columns),
@@ -535,7 +536,8 @@
     jb_irrep = lax.dynamic_slice_in_dim(occ_irrep, j_first, j_width, 0)[:, None] ^ virt_irrep[None, :]
     allowed = kc_irrep[:, None] == jb_irrep.reshape(1, -1)
     masked = jnp.where(allowed, gathered, jnp.zeros((), gathered.dtype))
-    return jnp.dot(amp, masked, preferred_element_type=jnp.float32)
+    cycle = jnp.dot(amp, masked, preferred_element_type=jnp.float32)
+    return cycle.reshape(amp.shape[0] // AW, AW // 8, 8, -1)
 
 
 def per_device(lam, ladder_int, cycle_amp, cycle_int, occ_irrep, virt_irrep):
@@ -577,8 +579,8 @@
             last = merge_z(kept[n], sent[n], last)
             second[n] = [exchange(last)]
         else:
-            last, keep = merge_x(sent[n], tiles[n] // LANES, last)
-            second[n] = [keep, swap(last, "z_hi")]
+            send, last = merge_x(sent[n], tiles[n] // LANES, last)
+            second[n] = [last, swap(send, "z_hi")]
         return last
 
     for step in ORDER:

time: 106 us -> 103 us (0.972)
  waiting for transfers between devices: 18 us -> 22.1 us
  local copies, waits for them, and re-layouts: 3.9 us -> 0.61 us
  Pallas kernels: 53.4 us -> 50.7 us
    cond x3 -> x2, local copies, waits for them, and re-layouts: 2.9 us -> 0.59 us
    ppermute x4, waiting for transfers between devices: 9.67 us -> 11.6 us  [swap(): return lax.ppermute(value, axis, [(0, 1), (1, 0)])]
    pallas_call x1, Pallas kernels: 3.43 us -> 1.81 us  [merge_z(): pl.pallas_call(merge_z_kernel, grid=(tiles,), in_specs=[WHOLE, WHOLE, ANY...]
    all_to_all x2, waiting for transfers between devices: 3.41 us -> 4.74 us  [exchange(): return lax.all_to_all(value, 'x', 0, 0)]
  transfers between devices with their start and end apart: 7 -> 7, of which waited for: 5 -> 5; matrix products, arithmetic and copies ran while one was open for 3% -> 1% of each run, Pallas kernels for 42% -> 42%
where the time goes in v3:
time: 103 us
  Pallas kernels  50.7 us (49%)
  waiting for transfers between devices  22.1 us (21%)
  starting transfers between devices  14.4 us (14%)
  between operations  14.1 us (14%)
    ppermute x4, waiting for transfers between devices, swap(): return lax.ppermute(value, axis, [(0, 1), (1, 0)])  11.6 us
    pallas_call x1, Pallas kernels, cycle_term(): pl.pallas_call(cycle_kernel, grid=(steps,), in_specs=[SCALARS, SCALARS, W...  10.4 us
    pallas_call x1, Pallas kernels, first_partner_part(): pl.pallas_call(first_partner_kernel, grid=(tiles,), in_specs=[pl.BlockSpe...  10.1 us
    all_to_all x2, starting transfers between devices, exchange(): return lax.all_to_all(value, 'x', 0, 0)  8.63 us
    pallas_call x1, Pallas kernels, own_x_part(): pl.pallas_call(own_x_kernel, grid=(tiles,), in_specs=[WHOLE, pl.BlockSpec...  8.38 us
    pallas_call x1, Pallas kernels, own_z_part(): pl.pallas_call(own_z_kernel, grid=(tiles,), in_specs=[pl.BlockSpec((rows,...  7.61 us
    ppermute x4, starting transfers between devices, swap(): return lax.ppermute(value, axis, [(0, 1), (1, 0)])  5.77 us
    all_gather x1, waiting for transfers between devices, per_device(): gathered = lax.all_gather(last, OCC, axis=0, tiled=True)  5.7 us
  transfers between devices with their start and end apart: 7, of which 5 were waited for; matrix products, arithmetic and copies ran while one was open for 1% of the time, Pallas kernels for 42%

profile of v3, /device:TPU:0, one launch (start us, length us, event | category | flops | bytes accessed | tf_op | source)
XLA Modules:
  0.0 102.7 jit_solution(16618544807084558289)
XLA Ops:
  6.5 0.0 all-gather.5.cloned.1.call-start
  6.5 3.0 %pack.1 = (bf16[400,512]{1,0:T(8,128)(2,1)}, s32[1,2048]{1,0:T(1,128)}) custom-call(s32[200]{0:T(256)} %occ_s_ref.1, s32[1,200]{1,0:T(1,128)} %bitcast.14, s32[1,256]{1,0:T(1,128)} %bitcast.12, bf16[400,2048]{1,0:T(8,128)(2,1)} %cycle_ref.1), custom_call_target="tpu_custom_call" | custom-call | flops 26214400 | bytes 78337 | tf_op jit(solution)/shard_map/pack/pallas_call | solution.py:447
  9.5 0.0 all-gather.5.cloned.1.call-update
  9.6 0.0 copy-start
  9.6 10.1 %partner_part.2 = (s16[2,5136,128]{2,1,0:T(8,128)(2,1)S(1)}, bf16[512,1792]{1,0:T(8,128)(2,1)S(1)}, bf16[512,1792]{1,0:T(8,128)(2,1)S(1)}) custom-call(bf16[1024,1792]{1,0:T(8,128)(2,1)} %lam_ref.1, bf16[1792,4096]{1,0:T(8,128)(2,1)} %panel_ref.7, bf16[400,512]{1,0:T(8,128)(2,1)} %get-tuple-element.50._), custom_call_target="tpu_custom_call" | custom-call | flops 587202560 | bytes 1376257 | tf_op jit(solution)/shard_map/partner_part/pallas_call | solution.py:111
  19.7 0.0 copy-start.1
  19.7 0.1 collective-permute-start
  19.8 0.0 copy-done
  19.8 5.2 %partner_part.3._ = s16[3,2064,128]{2,1,0:T(8,128)(2,1)} custom-call(bf16[512,1792]{1,0:T(8,128)(2,1)S(1)} %get-tuple-element.53.lam_ref, bf16[1792,4096]{1,0:T(8,128)(2,1)S(1)} %copy-done, s16[2,5136,128]{2,1,0:T(8,128)(2,1)S(1)} %get-tuple-element.52._), custom_call_target="tpu_custom_call" | custom-call | flops 352321536 | bytes 917505 | tf_op jit(solution)/shard_map/partner_part/pallas_call | solution.py:143
  25.0 0.5 collective-permute-start.1
  25.5 0.0 collective-permute-done.recv_ref
  25.5 0.0 copy-done.1
  25.5 8.4 %own_x_part.1._ = s16[4,2,1296,128]{3,2,1,0:T(8,128)(2,1)} custom-call(bf16[512,1792]{1,0:T(8,128)(2,1)S(1)} %get-tuple-element.51.lam_ref, bf16[1792,4096]{1,0:T(8,128)(2,1)S(1)} %copy-done, s16[2,5136,128]{2,1,0:T(8,128)(2,1)S(1)} %collective-permute-done.recv_ref, s16[3,2064,128]{2,1,0:T(8,128)(2,1)} %partner_part.3._), custom_call_target="tpu_custom_call" | custom-call | flops 587202560 | bytes 1376257 | tf_op jit(solution)/shard_map/own_x_part/pallas_call | solution.py:238
  33.9 4.4 %all-to-all-start = ((s16[4,2,1296,128]{3,2,1,0:T(8,128)(2,1)}), s16[4,2,1296,128]{3,2,1,0:T(8,128)(2,1)S(1)}, u32[]{:S(2)}, u32[]{:S(2)}) async-start(s16[4,2,1296,128]{3,2,1,0:T(8,128)(2,1)} %own_x_part.1._), calls=%async_computation | async-start | bytes 5308416 | tf_op jit(solution)/shard_map/all_to_all | solution.py:530
  38.2 0.0 copy-start.4
  38.2 0.0 collective-permute-done.1.recv_ref
  38.2 7.6 %own_z_part.1 = (s16[3,1040,128]{2,1,0:T(8,128)(2,1)}, f32[3,4,256,128]{3,2,1,0:T(8,128)}) custom-call(bf16[512,1792]{1,0:T(8,128)(2,1)} %copy-done.1, bf16[1792,4096]{1,0:T(8,128)(2,1)} %panel_ref.7, s16[3,2064,128]{2,1,0:T(8,128)(2,1)} %collective-permute-done.1.recv_ref, s16[4,2,1296,128]{3,2,1,0:T(8,128)(2,1)} %own_x_part.1._), custom_call_target="tpu_custom_call" | custom-call | flops 352321536 | bytes 917505 | tf_op jit(solution)/shard_map/own_z_part/pallas_call | solution.py:198
  45.9 3.9 %collective-permute-start.3 = (s16[3,1040,128]{2,1,0:T(8,128)(2,1)}, s16[3,1040,128]{2,1,0:T(8,128)(2,1)S(1)}, u32[]{:S(2)}, u32[]{:S(2)}) collective-permute-start(s16[3,1040,128]{2,1,0:T(8,128)(2,1)} %get-tuple-element.55), channel_id=1, source_target_pairs={{0,2},{2,0},{1,3},{3,1},{4,6},{6,4},{5,7},{7,5},{8,10},{10,8},{9,1... | collective-permute-start | bytes 2396168 | tf_op jit(solution)/shard_map/ppermute | solution.py:526
  49.7 0.0 copy-done.4
  49.7 0.8 compare_reduce_fusion
  51.2 5.7 %all-gather.5.cloned.1.call-done = bf16[3200,512]{1,0:T(8,128)(2,1)} async-done(((bf16[400,512]{1,0:T(8,128)(2,1)}), bf16[3200,512]{1,0:T(8,128)(2,1)}) %all-gather.5.cloned.1.call-update) | async-done | bytes 3276816 | tf_op jit(solution)/shard_map/all_gather | solution.py:548
  56.9 11.0 %conditional.1 = (f32[8,2,8,2048]{3,2,1,0:T(8,128)}) conditional(s32[]{:T(128)} %convert_element_type.3, (s32[200]{0:T(256)}, s32[256]{0:T(256)S(1)}, s32[]{:T(128)}, bf16[400,2048]{1,0:T(8,128)(2,1)}, bf16[128,3200]{1,0:T(8,128)(2,1)}, /*index=5*/(), s32[]{:T(128)}, s32[]{:T(128)}, (), ()) %tuple.28, (s32[256]{0:T(256)S(1)}, s32[200]{0:T(256)}, ...), branch_computations={%region_1.2_spmd, %region_2.3_spmd} | conditional | flops 1690834048 | bytes 59298000 | solution.py:588
  56.9 0.0 copy-start.5
  56.9 0.6 copy-done.5
  57.5 10.4 %cycle_term.1 = f32[8,2,8,2048]{3,2,1,0:T(8,128)} custom-call(s32[200]{0:T(256)} %get-tuple-element.35.occ_s_ref, s32[256]{0:T(256)} %copy-done.5, s32[1,256]{1,0:T(1,128)} %bitcast.13, s32[1,2048]{1,0:T(1,128)} %get-tuple-element.37.jb_ref, bf16[128,3200]{1,0:T(8,128)(2,1)} %get-tuple-element.38.amp_ref, bf16[3200,512]{1,0:T(8,128)(2,1)} %get-tuple-element.39.packed_ref, ...), custom_call_target="tpu_custom_call" | custom-call | flops 419430400 | bytes 1843201 | tf_op jit(solution)/shard_map/cond/branch_1_fun/cycle_term/pallas_call | solution.py:504
  68.0 2.8 %all-to-all-done.recv_ref = s16[4,2,1296,128]{3,2,1,0:T(8,128)(2,1)S(1)} async-done(((s16[4,2,1296,128]{3,2,1,0:T(8,128)(2,1)}), s16[4,2,1296,128]{3,2,1,0:T(8,128)(2,1)S(1)}, u32[]{:S(2)}, u32[]{:S(2)}) %all-to-all-start) | async-done | bytes 2654240 | tf_op jit(solution)/shard_map/all_to_all | solution.py:530
  70.7 0.0 copy-start.2
  70.7 1.7 %merge_x.1 = (s16[2,656,128]{2,1,0:T(8,128)(2,1)}, f32[2,10,64,128]{3,2,1,0:T(8,128)}) custom-call(s16[4,2,1296,128]{3,2,1,0:T(8,128)(2,1)S(1)} %all-to-all-done.recv_ref, f32[8,2,8,2048]{3,2,1,0:T(8,128)} %get-tuple-element.69._.refs_3_), custom_call_target="tpu_custom_call" | custom-call | bytes 331777 | tf_op jit(solution)/shard_map/merge_x/pallas_call | solution.py:316
  72.4 0.0 copy-start.6
  72.4 0.0 copy-start.3
  72.4 1.9 %collective-permute-done.3.recv_ref = s16[3,1040,128]{2,1,0:T(8,128)(2,1)S(1)} collective-permute-done((s16[3,1040,128]{2,1,0:T(8,128)(2,1)}, s16[3,1040,128]{2,1,0:T(8,128)(2,1)S(1)}, u32[]{:S(2)}, u32[]{:S(2)}) %collective-permute-start.3) | collective-permute-done | bytes 798752 | tf_op jit(solution)/shard_map/ppermute | solution.py:526
  74.3 0.0 copy-done.2
  74.3 1.8 %merge_z.1 = s16[4,3,272,128]{3,2,1,0:T(8,128)(2,1)} custom-call(f32[3,4,256,128]{3,2,1,0:T(8,128)S(1)} %copy-done.2, s16[3,1040,128]{2,1,0:T(8,128)(2,1)S(1)} %collective-permute-done.3.recv_ref, f32[2,10,64,128]{3,2,1,0:T(8,128)} %get-tuple-element.56._.refs_0_), custom_call_target="tpu_custom_call" | custom-call | bytes 394753 | tf_op jit(solution)/shard_map/merge_z/pallas_call | solution.py:277
  76.2 4.2 %all-to-all-start.1 = ((s16[4,3,272,128]{3,2,1,0:T(8,128)(2,1)}), s16[4,3,272,128]{3,2,1,0:T(8,128)(2,1)S(1)}, u32[]{:S(2)}, u32[]{:S(2)}) async-start(s16[4,3,272,128]{3,2,1,0:T(8,128)(2,1)} %merge_z.1), calls=%async_computation.1 | async-start | bytes 1671168 | tf_op jit(solution)/shard_map/all_to_all | solution.py:530
  80.4 0.0 copy-done.6
  80.4 1.3 %collective-permute-start.2 = (s16[2,656,128]{2,1,0:T(8,128)(2,1)S(1)}, s16[2,656,128]{2,1,0:T(8,128)(2,1)S(1)}, u32[]{:S(2)}, u32[]{:S(2)}) collective-permute-start(s16[2,656,128]{2,1,0:T(8,128)(2,1)S(1)} %copy-done.6), channel_id=1, source_target_pairs={{0,2},{2,0},{1,3},{3,1},{4,6},{6,4},{5,7},{7,5},{8,10},{10,8},{9,1... | collective-permute-start | bytes 1007624 | tf_op jit(solution)/shard_map/ppermute | solution.py:526
  81.7 9.7 %collective-permute-done.2.refs_1_ = s16[2,656,128]{2,1,0:T(8,128)(2,1)S(1)} collective-permute-done((s16[2,656,128]{2,1,0:T(8,128)(2,1)S(1)}, s16[2,656,128]{2,1,0:T(8,128)(2,1)S(1)}, u32[]{:S(2)}, u32[]{:S(2)}) %collective-permute-start.2) | collective-permute-done | bytes 335904 | tf_op jit(solution)/shard_map/ppermute | solution.py:526
  91.4 2.0 %all-to-all-done.1.refs_2_ = s16[4,3,272,128]{3,2,1,0:T(8,128)(2,1)S(1)} async-done(((s16[4,3,272,128]{3,2,1,0:T(8,128)(2,1)}), s16[4,3,272,128]{3,2,1,0:T(8,128)(2,1)S(1)}, u32[]{:S(2)}, u32[]{:S(2)}) %all-to-all-start.1) | async-done | bytes 835616 | tf_op jit(solution)/shard_map/all_to_all | solution.py:530
  93.4 0.0 copy-done.3
  93.4 2.5 %finish.1 = f32[8,2,8,2048]{3,2,1,0:T(8,128)} custom-call(f32[2,10,64,128]{3,2,1,0:T(8,128)} %get-tuple-element.56._.refs_0_, s16[2,656,128]{2,1,0:T(8,128)(2,1)S(1)} %collective-permute-done.2.refs_1_, s16[4,3,272,128]{3,2,1,0:T(8,128)(2,1)S(1)} %all-to-all-done.1.refs_2_, f32[8,2,8,2048]{3,2,1,0:T(8,128)S(1)} %copy-done.3), custom_call_target="tpu_custom_call" | custom-call | bytes 524289 | tf_op jit(solution)/shard_map/finish/pallas_call | solution.py:387
Async XLA Ops:
  6.5 50.4 %all-gather.5.cloned.1.call-start = ((), (), s32[]{:S(2)}) async-start(), calls=%async_computation.3 | async-start | bytes 3686400 | tf_op jit(solution)/shard_map/all_gather | solution.py:548
  9.6 10.2 %copy-start = (bf16[1792,4096]{1,0:T(8,128)(2,1)S(1)}, bf16[1792,4096]{1,0:T(8,128)(2,1)}, u32[]{:S(2)}) copy-start(bf16[1792,4096]{1,0:T(8,128)(2,1)} %panel_ref.7) | copy-start | bytes 44040196
  19.7 5.8 %copy-start.1 = (bf16[512,1792]{1,0:T(8,128)(2,1)}, bf16[512,1792]{1,0:T(8,128)(2,1)S(1)}, u32[]{:S(2)}) copy-start(bf16[512,1792]{1,0:T(8,128)(2,1)S(1)} %get-tuple-element.51.lam_ref) | copy-start | bytes 5505028
  19.7 5.8 %collective-permute-start = (s16[2,5136,128]{2,1,0:T(8,128)(2,1)S(1)}, s16[2,5136,128]{2,1,0:T(8,128)(2,1)S(1)}, u32[]{:S(2)}, u32[]{:S(2)}) collective-permute-start(s16[2,5136,128]{2,1,0:T(8,128)(2,1)S(1)} %get-tuple-element.52._), channel_id=1, source_target_pairs={{0,1},{1,0},{2,3},{3,2},{4,5},{5,4},{6,7},{7,6},{8,9},{9,8},{10,11... | collective-permute-start | bytes 7888904 | tf_op jit(solution)/shard_map/ppermute | solution.py:526
  25.0 13.2 %collective-permute-start.1 = (s16[3,2064,128]{2,1,0:T(8,128)(2,1)}, s16[3,2064,128]{2,1,0:T(8,128)(2,1)}, u32[]{:S(2)}, u32[]{:S(2)}) collective-permute-start(s16[3,2064,128]{2,1,0:T(8,128)(2,1)} %partner_part.3._), channel_id=1, source_target_pairs={{0,1},{1,0},{2,3},{3,2},{4,5},{5,4},{6,7},{7,6},{8,9},{9,8},{10,11... | collective-permute-start | bytes 4755464 | tf_op jit(solution)/shard_map/ppermute | solution.py:526
  33.9 36.9 %all-to-all-start = ((s16[4,2,1296,128]{3,2,1,0:T(8,128)(2,1)}), s16[4,2,1296,128]{3,2,1,0:T(8,128)(2,1)S(1)}, u32[]{:S(2)}, u32[]{:S(2)}) async-start(s16[4,2,1296,128]{3,2,1,0:T(8,128)(2,1)} %own_x_part.1._), calls=%async_computation | async-start | bytes 5308416 | tf_op jit(solution)/shard_map/all_to_all | solution.py:530
  38.2 11.5 %copy-start.4 = (s32[256]{0:T(256)S(1)}, s32[256]{0:T(256)}, u32[]{:S(2)}) copy-start(s32[256]{0:T(256)} %param.13) | copy-start | bytes 3076
  45.9 28.5 %collective-permute-start.3 = (s16[3,1040,128]{2,1,0:T(8,128)(2,1)}, s16[3,1040,128]{2,1,0:T(8,128)(2,1)S(1)}, u32[]{:S(2)}, u32[]{:S(2)}) collective-permute-start(s16[3,1040,128]{2,1,0:T(8,128)(2,1)} %get-tuple-element.55), channel_id=1, source_target_pairs={{0,2},{2,0},{1,3},{3,1},{4,6},{6,4},{5,7},{7,5},{8,10},{10,8},{9,1... | collective-permute-start | bytes 2396168 | tf_op jit(solution)/shard_map/ppermute | solution.py:526
  56.9 0.6 copy-start.5
  70.7 3.6 %copy-start.2 = (f32[3,4,256,128]{3,2,1,0:T(8,128)S(1)}, f32[3,4,256,128]{3,2,1,0:T(8,128)}, u32[]{:S(2)}) copy-start(f32[3,4,256,128]{3,2,1,0:T(8,128)} %get-tuple-element.58.keep_ref) | copy-start | bytes 4718596
  72.4 8.0 %copy-start.6 = (s16[2,656,128]{2,1,0:T(8,128)(2,1)S(1)}, s16[2,656,128]{2,1,0:T(8,128)(2,1)}, u32[]{:S(2)}) copy-start(s16[2,656,128]{2,1,0:T(8,128)(2,1)} %get-tuple-element.57) | copy-start | bytes 1007620
  72.4 21.0 %copy-start.3 = (f32[8,2,8,2048]{3,2,1,0:T(8,128)S(1)}, f32[8,2,8,2048]{3,2,1,0:T(8,128)}, u32[]{:S(2)}) copy-start(f32[8,2,8,2048]{3,2,1,0:T(8,128)} %get-tuple-element.69._.refs_3_) | copy-start | bytes 3145732
  76.2 17.2 %all-to-all-start.1 = ((s16[4,3,272,128]{3,2,1,0:T(8,128)(2,1)}), s16[4,3,272,128]{3,2,1,0:T(8,128)(2,1)S(1)}, u32[]{:S(2)}, u32[]{:S(2)}) async-start(s16[4,3,272,128]{3,2,1,0:T(8,128)(2,1)} %merge_z.1), calls=%async_computation.1 | async-start | bytes 1671168 | tf_op jit(solution)/shard_map/all_to_all | solution.py:530
  80.4 11.0 %collective-permute-start.2 = (s16[2,656,128]{2,1,0:T(8,128)(2,1)S(1)}, s16[2,656,128]{2,1,0:T(8,128)(2,1)S(1)}, u32[]{:S(2)}, u32[]{:S(2)}) collective-permute-start(s16[2,656,128]{2,1,0:T(8,128)(2,1)S(1)} %copy-done.6), channel_id=1, source_target_pairs={{0,2},{2,0},{1,3},{3,1},{4,6},{6,4},{5,7},{7,5},{8,10},{10,8},{9,1... | collective-permute-start | bytes 1007624 | tf_op jit(solution)/shard_map/ppermute | solution.py:526
Sparse Core Ops, SparseCore 0:
  9.7 47.1 all-gather.4

commit v4 on v3

--- a/solution.py
+++ b/solution.py
@@ -424,18 +424,28 @@
     return k_label ^ c_label
 
 
-def pack_kernel(occ_s_ref, occ_ref, virt_ref, cycle_ref, packed_ref, jb_ref):
-    rows, columns = cycle_ref.shape
+def pack_kernel(occ_s_ref, occ_ref, virt_ref, cycle_ref, packed_ref, jb_ref, held_ref, sems):
+    rows, columns = held_ref.shape
+    width = LANES // SEGMENT * BW
+    steps = columns // width
+    copies = [
+        pltpu.make_async_copy(
+            cycle_ref.at[:, pl.ds(step * width, width)], held_ref.at[:, pl.ds(step * width, width)], sems.at[step]
+        )
+        for step in range(steps)
+    ]
+    for copy in copies:
+        copy.start()
     virt = virt_ref[...]
     mine = row_labels(occ_ref[...], virt, lax.axis_index(OCC) * (rows // PAN), rows)
     spread = spread_matrix(virt)
-    width = spread.shape[1]
-    for step in range(columns // width):
+    for step in range(steps):
         lanes = slice(step * width, (step + 1) * width)
-        first = (lax.axis_index(VIR) * (columns // width) + step) * (width // BW)
+        first = (lax.axis_index(VIR) * steps + step) * (width // BW)
         jb = jnp.concatenate([virt ^ occ_s_ref[first + jj] for jj in range(width // BW)], axis=1)
         jb_ref[:, lanes] = jb
-        masked = jnp.where(mine == jb, cycle_ref[:, lanes].astype(jnp.float32), 0.0).astype(jnp.bfloat16)
+        copies[step].wait()
+        masked = jnp.where(mine == jb, held_ref[:, lanes].astype(jnp.float32), 0.0).astype(jnp.bfloat16)
         packed_ref[:, step * LANES : (step + 1) * LANES] = lax.dot_general(
             masked, spread, (((1,), (1,)), ((), ())), preferred_element_type=jnp.float32
         ).astype(jnp.bfloat16)
@@ -446,10 +456,14 @@
     width = columns * SEGMENT // BW
     return pl.pallas_call(
         pack_kernel,
-        in_specs=[SCALARS, WHOLE, WHOLE, WHOLE],
+        in_specs=[SCALARS, WHOLE, WHOLE, ANYWHERE],
         out_shape=[
             jax.ShapeDtypeStruct((rows, width), jnp.bfloat16),
             jax.ShapeDtypeStruct((1, columns), jnp.int32),
+        ],
+        scratch_shapes=[
+            pltpu.VMEM((rows, columns), jnp.bfloat16),
+            pltpu.SemaphoreType.DMA((columns * SEGMENT // BW // LANES,)),
         ],
         compiler_params=params(12),
         cost_estimate=cost(rows, LANES, columns),

time: 103 us -> 104 us (level)
  no operation moved by 1% of the time
where the time goes in v4:
time: 104 us
  Pallas kernels  51.6 us (50%)
  waiting for transfers between devices  22.1 us (21%)
  starting transfers between devices  14.4 us (14%)
  between operations  14.1 us (14%)
    ppermute x4, waiting for transfers between devices, swap(): return lax.ppermute(value, axis, [(0, 1), (1, 0)])  11.7 us
    pallas_call x1, Pallas kernels, cycle_term(): pl.pallas_call(cycle_kernel, grid=(steps,), in_specs=[SCALARS, SCALARS, W...  10.5 us
    pallas_call x1, Pallas kernels, first_partner_part(): pl.pallas_call(first_partner_kernel, grid=(tiles,), in_specs=[pl.BlockSpe...  10.1 us
    all_to_all x2, starting transfers between devices, exchange(): return lax.all_to_all(value, 'x', 0, 0)  8.63 us
    pallas_call x1, Pallas kernels, own_x_part(): pl.pallas_call(own_x_kernel, grid=(tiles,), in_specs=[WHOLE, pl.BlockSpec...  8.38 us
    pallas_call x1, Pallas kernels, own_z_part(): pl.pallas_call(own_z_kernel, grid=(tiles,), in_specs=[pl.BlockSpec((rows,...  7.62 us
    ppermute x4, starting transfers between devices, swap(): return lax.ppermute(value, axis, [(0, 1), (1, 0)])  5.76 us
    all_gather x1, waiting for transfers between devices, per_device(): gathered = lax.all_gather(last, OCC, axis=0, tiled=True)  5.71 us
  transfers between devices with their start and end apart: 7, of which 5 were waited for; matrix products, arithmetic and copies ran while one was open for 1% of the time, Pallas kernels for 42%

profile of v4, /device:TPU:0, one launch (start us, length us, event | category | flops | bytes accessed | tf_op | source)
XLA Modules:
  0.0 103.6 jit_solution(14949317415755606637)
XLA Ops:
  6.5 0.0 all-gather.5.cloned.1.call-start
  6.5 3.9 %pack.1 = (bf16[400,512]{1,0:T(8,128)(2,1)}, s32[1,2048]{1,0:T(1,128)}) custom-call(s32[200]{0:T(256)} %occ_s_ref.1, s32[1,200]{1,0:T(1,128)} %bitcast.14, s32[1,256]{1,0:T(1,128)} %bitcast.12, bf16[400,2048]{1,0:T(8,128)(2,1)} %cycle_ref.1), custom_call_target="tpu_custom_call" | custom-call | flops 26214400 | bytes 78337 | tf_op jit(solution)/shard_map/pack/pallas_call | solution.py:457
  10.4 0.0 all-gather.5.cloned.1.call-update
  10.5 0.0 copy-start
  10.5 10.1 %partner_part.2 = (s16[2,5136,128]{2,1,0:T(8,128)(2,1)S(1)}, bf16[512,1792]{1,0:T(8,128)(2,1)S(1)}, bf16[512,1792]{1,0:T(8,128)(2,1)S(1)}) custom-call(bf16[1024,1792]{1,0:T(8,128)(2,1)} %lam_ref.1, bf16[1792,4096]{1,0:T(8,128)(2,1)} %panel_ref.7, bf16[400,512]{1,0:T(8,128)(2,1)} %get-tuple-element.50._), custom_call_target="tpu_custom_call" | custom-call | flops 587202560 | bytes 1376257 | tf_op jit(solution)/shard_map/partner_part/pallas_call | solution.py:111
  20.6 0.0 copy-start.1
  20.6 0.1 collective-permute-start
  20.7 0.0 copy-done
  20.7 5.2 %partner_part.3._ = s16[3,2064,128]{2,1,0:T(8,128)(2,1)} custom-call(bf16[512,1792]{1,0:T(8,128)(2,1)S(1)} %get-tuple-element.53.lam_ref, bf16[1792,4096]{1,0:T(8,128)(2,1)S(1)} %copy-done, s16[2,5136,128]{2,1,0:T(8,128)(2,1)S(1)} %get-tuple-element.52._), custom_call_target="tpu_custom_call" | custom-call | flops 352321536 | bytes 917505 | tf_op jit(solution)/shard_map/partner_part/pallas_call | solution.py:143
  25.9 0.5 collective-permute-start.1
  26.4 0.0 collective-permute-done.recv_ref
  26.4 0.0 copy-done.1
  26.4 8.4 %own_x_part.1._ = s16[4,2,1296,128]{3,2,1,0:T(8,128)(2,1)} custom-call(bf16[512,1792]{1,0:T(8,128)(2,1)S(1)} %get-tuple-element.51.lam_ref, bf16[1792,4096]{1,0:T(8,128)(2,1)S(1)} %copy-done, s16[2,5136,128]{2,1,0:T(8,128)(2,1)S(1)} %collective-permute-done.recv_ref, s16[3,2064,128]{2,1,0:T(8,128)(2,1)} %partner_part.3._), custom_call_target="tpu_custom_call" | custom-call | flops 587202560 | bytes 1376257 | tf_op jit(solution)/shard_map/own_x_part/pallas_call | solution.py:238
  34.7 4.4 %all-to-all-start = ((s16[4,2,1296,128]{3,2,1,0:T(8,128)(2,1)}), s16[4,2,1296,128]{3,2,1,0:T(8,128)(2,1)S(1)}, u32[]{:S(2)}, u32[]{:S(2)}) async-start(s16[4,2,1296,128]{3,2,1,0:T(8,128)(2,1)} %own_x_part.1._), calls=%async_computation | async-start | bytes 5308416 | tf_op jit(solution)/shard_map/all_to_all | solution.py:544
  39.1 0.0 copy-start.4
  39.1 0.0 collective-permute-done.1.recv_ref
  39.1 7.6 %own_z_part.1 = (s16[3,1040,128]{2,1,0:T(8,128)(2,1)}, f32[3,4,256,128]{3,2,1,0:T(8,128)}) custom-call(bf16[512,1792]{1,0:T(8,128)(2,1)} %copy-done.1, bf16[1792,4096]{1,0:T(8,128)(2,1)} %panel_ref.7, s16[3,2064,128]{2,1,0:T(8,128)(2,1)} %collective-permute-done.1.recv_ref, s16[4,2,1296,128]{3,2,1,0:T(8,128)(2,1)} %own_x_part.1._), custom_call_target="tpu_custom_call" | custom-call | flops 352321536 | bytes 917505 | tf_op jit(solution)/shard_map/own_z_part/pallas_call | solution.py:198
  46.8 3.9 %collective-permute-start.3 = (s16[3,1040,128]{2,1,0:T(8,128)(2,1)}, s16[3,1040,128]{2,1,0:T(8,128)(2,1)S(1)}, u32[]{:S(2)}, u32[]{:S(2)}) collective-permute-start(s16[3,1040,128]{2,1,0:T(8,128)(2,1)} %get-tuple-element.55), channel_id=1, source_target_pairs={{0,2},{2,0},{1,3},{3,1},{4,6},{6,4},{5,7},{7,5},{8,10},{10,8},{9,1... | collective-permute-start | bytes 2396168 | tf_op jit(solution)/shard_map/ppermute | solution.py:540
  50.6 0.0 copy-done.4
  50.6 0.8 compare_reduce_fusion
  52.1 5.7 %all-gather.5.cloned.1.call-done = bf16[3200,512]{1,0:T(8,128)(2,1)} async-done(((bf16[400,512]{1,0:T(8,128)(2,1)}), bf16[3200,512]{1,0:T(8,128)(2,1)}) %all-gather.5.cloned.1.call-update) | async-done | bytes 3276816 | tf_op jit(solution)/shard_map/all_gather | solution.py:562
  57.8 11.0 %conditional.1 = (f32[8,2,8,2048]{3,2,1,0:T(8,128)}) conditional(s32[]{:T(128)} %convert_element_type.3, (s32[200]{0:T(256)}, s32[256]{0:T(256)S(1)}, s32[]{:T(128)}, bf16[400,2048]{1,0:T(8,128)(2,1)}, bf16[128,3200]{1,0:T(8,128)(2,1)}, /*index=5*/(), s32[]{:T(128)}, s32[]{:T(128)}, (), ()) %tuple.28, (s32[256]{0:T(256)S(1)}, s32[200]{0:T(256)}, ...), branch_computations={%region_1.2_spmd, %region_2.3_spmd} | conditional | flops 1690834048 | bytes 59298000 | solution.py:602
  57.8 0.0 copy-start.5
  57.8 0.6 copy-done.5
  58.4 10.5 %cycle_term.1 = f32[8,2,8,2048]{3,2,1,0:T(8,128)} custom-call(s32[200]{0:T(256)} %get-tuple-element.35.occ_s_ref, s32[256]{0:T(256)} %copy-done.5, s32[1,256]{1,0:T(1,128)} %bitcast.13, s32[1,2048]{1,0:T(1,128)} %get-tuple-element.37.jb_ref, bf16[128,3200]{1,0:T(8,128)(2,1)} %get-tuple-element.38.amp_ref, bf16[3200,512]{1,0:T(8,128)(2,1)} %get-tuple-element.39.packed_ref, ...), custom_call_target="tpu_custom_call" | custom-call | flops 419430400 | bytes 1843201 | tf_op jit(solution)/shard_map/cond/branch_1_fun/cycle_term/pallas_call | solution.py:518
  68.9 2.8 %all-to-all-done.recv_ref = s16[4,2,1296,128]{3,2,1,0:T(8,128)(2,1)S(1)} async-done(((s16[4,2,1296,128]{3,2,1,0:T(8,128)(2,1)}), s16[4,2,1296,128]{3,2,1,0:T(8,128)(2,1)S(1)}, u32[]{:S(2)}, u32[]{:S(2)}) %all-to-all-start) | async-done | bytes 2654240 | tf_op jit(solution)/shard_map/all_to_all | solution.py:544
  71.6 0.0 copy-start.2
  71.6 1.7 %merge_x.1 = (s16[2,656,128]{2,1,0:T(8,128)(2,1)}, f32[2,10,64,128]{3,2,1,0:T(8,128)}) custom-call(s16[4,2,1296,128]{3,2,1,0:T(8,128)(2,1)S(1)} %all-to-all-done.recv_ref, f32[8,2,8,2048]{3,2,1,0:T(8,128)} %get-tuple-element.69._.refs_3_), custom_call_target="tpu_custom_call" | custom-call | bytes 331777 | tf_op jit(solution)/shard_map/merge_x/pallas_call | solution.py:316
  73.3 0.0 copy-start.6
  73.3 0.0 copy-start.3
  73.3 1.9 %collective-permute-done.3.recv_ref = s16[3,1040,128]{2,1,0:T(8,128)(2,1)S(1)} collective-permute-done((s16[3,1040,128]{2,1,0:T(8,128)(2,1)}, s16[3,1040,128]{2,1,0:T(8,128)(2,1)S(1)}, u32[]{:S(2)}, u32[]{:S(2)}) %collective-permute-start.3) | collective-permute-done | bytes 798752 | tf_op jit(solution)/shard_map/ppermute | solution.py:540
  75.2 0.0 copy-done.2
  75.2 1.8 %merge_z.1 = s16[4,3,272,128]{3,2,1,0:T(8,128)(2,1)} custom-call(f32[3,4,256,128]{3,2,1,0:T(8,128)S(1)} %copy-done.2, s16[3,1040,128]{2,1,0:T(8,128)(2,1)S(1)} %collective-permute-done.3.recv_ref, f32[2,10,64,128]{3,2,1,0:T(8,128)} %get-tuple-element.56._.refs_0_), custom_call_target="tpu_custom_call" | custom-call | bytes 394753 | tf_op jit(solution)/shard_map/merge_z/pallas_call | solution.py:277
  77.1 4.2 %all-to-all-start.1 = ((s16[4,3,272,128]{3,2,1,0:T(8,128)(2,1)}), s16[4,3,272,128]{3,2,1,0:T(8,128)(2,1)S(1)}, u32[]{:S(2)}, u32[]{:S(2)}) async-start(s16[4,3,272,128]{3,2,1,0:T(8,128)(2,1)} %merge_z.1), calls=%async_computation.1 | async-start | bytes 1671168 | tf_op jit(solution)/shard_map/all_to_all | solution.py:544
  81.3 0.0 copy-done.6
  81.3 1.3 %collective-permute-start.2 = (s16[2,656,128]{2,1,0:T(8,128)(2,1)S(1)}, s16[2,656,128]{2,1,0:T(8,128)(2,1)S(1)}, u32[]{:S(2)}, u32[]{:S(2)}) collective-permute-start(s16[2,656,128]{2,1,0:T(8,128)(2,1)S(1)} %copy-done.6), channel_id=1, source_target_pairs={{0,2},{2,0},{1,3},{3,1},{4,6},{6,4},{5,7},{7,5},{8,10},{10,8},{9,1... | collective-permute-start | bytes 1007624 | tf_op jit(solution)/shard_map/ppermute | solution.py:540
  82.6 9.7 %collective-permute-done.2.refs_1_ = s16[2,656,128]{2,1,0:T(8,128)(2,1)S(1)} collective-permute-done((s16[2,656,128]{2,1,0:T(8,128)(2,1)S(1)}, s16[2,656,128]{2,1,0:T(8,128)(2,1)S(1)}, u32[]{:S(2)}, u32[]{:S(2)}) %collective-permute-start.2) | collective-permute-done | bytes 335904 | tf_op jit(solution)/shard_map/ppermute | solution.py:540
  92.3 2.0 %all-to-all-done.1.refs_2_ = s16[4,3,272,128]{3,2,1,0:T(8,128)(2,1)S(1)} async-done(((s16[4,3,272,128]{3,2,1,0:T(8,128)(2,1)}), s16[4,3,272,128]{3,2,1,0:T(8,128)(2,1)S(1)}, u32[]{:S(2)}, u32[]{:S(2)}) %all-to-all-start.1) | async-done | bytes 835616 | tf_op jit(solution)/shard_map/all_to_all | solution.py:544
  94.3 0.0 copy-done.3
  94.3 2.5 %finish.1 = f32[8,2,8,2048]{3,2,1,0:T(8,128)} custom-call(f32[2,10,64,128]{3,2,1,0:T(8,128)} %get-tuple-element.56._.refs_0_, s16[2,656,128]{2,1,0:T(8,128)(2,1)S(1)} %collective-permute-done.2.refs_1_, s16[4,3,272,128]{3,2,1,0:T(8,128)(2,1)S(1)} %all-to-all-done.1.refs_2_, f32[8,2,8,2048]{3,2,1,0:T(8,128)S(1)} %copy-done.3), custom_call_target="tpu_custom_call" | custom-call | bytes 524289 | tf_op jit(solution)/shard_map/finish/pallas_call | solution.py:387
Async XLA Ops:
  6.5 51.3 %all-gather.5.cloned.1.call-start = ((), (), s32[]{:S(2)}) async-start(), calls=%async_computation.3 | async-start | bytes 3686400 | tf_op jit(solution)/shard_map/all_gather | solution.py:562
  10.5 10.2 %copy-start = (bf16[1792,4096]{1,0:T(8,128)(2,1)S(1)}, bf16[1792,4096]{1,0:T(8,128)(2,1)}, u32[]{:S(2)}) copy-start(bf16[1792,4096]{1,0:T(8,128)(2,1)} %panel_ref.7) | copy-start | bytes 44040196
  20.6 5.8 %copy-start.1 = (bf16[512,1792]{1,0:T(8,128)(2,1)}, bf16[512,1792]{1,0:T(8,128)(2,1)S(1)}, u32[]{:S(2)}) copy-start(bf16[512,1792]{1,0:T(8,128)(2,1)S(1)} %get-tuple-element.51.lam_ref) | copy-start | bytes 5505028
  20.6 5.8 %collective-permute-start = (s16[2,5136,128]{2,1,0:T(8,128)(2,1)S(1)}, s16[2,5136,128]{2,1,0:T(8,128)(2,1)S(1)}, u32[]{:S(2)}, u32[]{:S(2)}) collective-permute-start(s16[2,5136,128]{2,1,0:T(8,128)(2,1)S(1)} %get-tuple-element.52._), channel_id=1, source_target_pairs={{0,1},{1,0},{2,3},{3,2},{4,5},{5,4},{6,7},{7,6},{8,9},{9,8},{10,11... | collective-permute-start | bytes 7888904 | tf_op jit(solution)/shard_map/ppermute | solution.py:540
  25.9 13.2 %collective-permute-start.1 = (s16[3,2064,128]{2,1,0:T(8,128)(2,1)}, s16[3,2064,128]{2,1,0:T(8,128)(2,1)}, u32[]{:S(2)}, u32[]{:S(2)}) collective-permute-start(s16[3,2064,128]{2,1,0:T(8,128)(2,1)} %partner_part.3._), channel_id=1, source_target_pairs={{0,1},{1,0},{2,3},{3,2},{4,5},{5,4},{6,7},{7,6},{8,9},{9,8},{10,11... | collective-permute-start | bytes 4755464 | tf_op jit(solution)/shard_map/ppermute | solution.py:540
  34.7 36.9 %all-to-all-start = ((s16[4,2,1296,128]{3,2,1,0:T(8,128)(2,1)}), s16[4,2,1296,128]{3,2,1,0:T(8,128)(2,1)S(1)}, u32[]{:S(2)}, u32[]{:S(2)}) async-start(s16[4,2,1296,128]{3,2,1,0:T(8,128)(2,1)} %own_x_part.1._), calls=%async_computation | async-start | bytes 5308416 | tf_op jit(solution)/shard_map/all_to_all | solution.py:544
  39.1 11.5 %copy-start.4 = (s32[256]{0:T(256)S(1)}, s32[256]{0:T(256)}, u32[]{:S(2)}) copy-start(s32[256]{0:T(256)} %param.13) | copy-start | bytes 3076
  46.8 28.5 %collective-permute-start.3 = (s16[3,1040,128]{2,1,0:T(8,128)(2,1)}, s16[3,1040,128]{2,1,0:T(8,128)(2,1)S(1)}, u32[]{:S(2)}, u32[]{:S(2)}) collective-permute-start(s16[3,1040,128]{2,1,0:T(8,128)(2,1)} %get-tuple-element.55), channel_id=1, source_target_pairs={{0,2},{2,0},{1,3},{3,1},{4,6},{6,4},{5,7},{7,5},{8,10},{10,8},{9,1... | collective-permute-start | bytes 2396168 | tf_op jit(solution)/shard_map/ppermute | solution.py:540
  57.8 0.6 copy-start.5
  71.6 3.6 %copy-start.2 = (f32[3,4,256,128]{3,2,1,0:T(8,128)S(1)}, f32[3,4,256,128]{3,2,1,0:T(8,128)}, u32[]{:S(2)}) copy-start(f32[3,4,256,128]{3,2,1,0:T(8,128)} %get-tuple-element.58.keep_ref) | copy-start | bytes 4718596
  73.3 8.0 %copy-start.6 = (s16[2,656,128]{2,1,0:T(8,128)(2,1)S(1)}, s16[2,656,128]{2,1,0:T(8,128)(2,1)}, u32[]{:S(2)}) copy-start(s16[2,656,128]{2,1,0:T(8,128)(2,1)} %get-tuple-element.57) | copy-start | bytes 1007620
  73.3 21.0 %copy-start.3 = (f32[8,2,8,2048]{3,2,1,0:T(8,128)S(1)}, f32[8,2,8,2048]{3,2,1,0:T(8,128)}, u32[]{:S(2)}) copy-start(f32[8,2,8,2048]{3,2,1,0:T(8,128)} %get-tuple-element.69._.refs_3_) | copy-start | bytes 3145732
  77.1 17.2 %all-to-all-start.1 = ((s16[4,3,272,128]{3,2,1,0:T(8,128)(2,1)}), s16[4,3,272,128]{3,2,1,0:T(8,128)(2,1)S(1)}, u32[]{:S(2)}, u32[]{:S(2)}) async-start(s16[4,3,272,128]{3,2,1,0:T(8,128)(2,1)} %merge_z.1), calls=%async_computation.1 | async-start | bytes 1671168 | tf_op jit(solution)/shard_map/all_to_all | solution.py:544
  81.3 11.0 %collective-permute-start.2 = (s16[2,656,128]{2,1,0:T(8,128)(2,1)S(1)}, s16[2,656,128]{2,1,0:T(8,128)(2,1)S(1)}, u32[]{:S(2)}, u32[]{:S(2)}) collective-permute-start(s16[2,656,128]{2,1,0:T(8,128)(2,1)S(1)} %copy-done.6), channel_id=1, source_target_pairs={{0,2},{2,0},{1,3},{3,1},{4,6},{6,4},{5,7},{7,5},{8,10},{10,8},{9,1... | collective-permute-start | bytes 1007624 | tf_op jit(solution)/shard_map/ppermute | solution.py:540
Sparse Core Ops, SparseCore 0:
  10.6 47.1 all-gather.4

commit v5 on v3

--- a/solution.py
+++ b/solution.py
@@ -435,7 +435,7 @@
         first = (lax.axis_index(VIR) * (columns // width) + step) * (width // BW)
         jb = jnp.concatenate([virt ^ occ_s_ref[first + jj] for jj in range(width // BW)], axis=1)
         jb_ref[:, lanes] = jb
-        masked = jnp.where(mine == jb, cycle_ref[:, lanes].astype(jnp.float32), 0.0).astype(jnp.bfloat16)
+        masked = jnp.where(mine == jb, cycle_ref[:, lanes], jnp.zeros((), jnp.bfloat16))
         packed_ref[:, step * LANES : (step + 1) * LANES] = lax.dot_general(
             masked, spread, (((1,), (1,)), ((), ())), preferred_element_type=jnp.float32
         ).astype(jnp.bfloat16)

time: 103 us -> 103 us (level)
  no operation moved by 1% of the time
where the time goes in v5:
time: 103 us
  Pallas kernels  50.7 us (49%)
  waiting for transfers between devices  22.1 us (21%)
  starting transfers between devices  14.4 us (14%)
  between operations  14.1 us (14%)
    ppermute x4, waiting for transfers between devices, swap(): return lax.ppermute(value, axis, [(0, 1), (1, 0)])  11.7 us
    pallas_call x1, Pallas kernels, cycle_term(): pl.pallas_call(cycle_kernel, grid=(steps,), in_specs=[SCALARS, SCALARS, W...  10.4 us
    pallas_call x1, Pallas kernels, first_partner_part(): pl.pallas_call(first_partner_kernel, grid=(tiles,), in_specs=[pl.BlockSpe...  10.1 us
    all_to_all x2, starting transfers between devices, exchange(): return lax.all_to_all(value, 'x', 0, 0)  8.63 us
    pallas_call x1, Pallas kernels, own_x_part(): pl.pallas_call(own_x_kernel, grid=(tiles,), in_specs=[WHOLE, pl.BlockSpec...  8.38 us
    pallas_call x1, Pallas kernels, own_z_part(): pl.pallas_call(own_z_kernel, grid=(tiles,), in_specs=[pl.BlockSpec((rows,...  7.61 us
    ppermute x4, starting transfers between devices, swap(): return lax.ppermute(value, axis, [(0, 1), (1, 0)])  5.76 us
    all_gather x1, waiting for transfers between devices, per_device(): gathered = lax.all_gather(last, OCC, axis=0, tiled=True)  5.71 us
  transfers between devices with their start and end apart: 7, of which 5 were waited for; matrix products, arithmetic and copies ran while one was open for 1% of the time, Pallas kernels for 42%

profile of v5, /device:TPU:0, one launch (start us, length us, event | category | flops | bytes accessed | tf_op | source)
XLA Modules:
  0.0 102.7 jit_solution(14209035385243070466)
XLA Ops:
  6.5 0.0 all-gather.5.cloned.1.call-start
  6.5 3.0 %pack.1 = (bf16[400,512]{1,0:T(8,128)(2,1)}, s32[1,2048]{1,0:T(1,128)}) custom-call(s32[200]{0:T(256)} %occ_s_ref.1, s32[1,200]{1,0:T(1,128)} %bitcast.14, s32[1,256]{1,0:T(1,128)} %bitcast.12, bf16[400,2048]{1,0:T(8,128)(2,1)} %cycle_ref.1), custom_call_target="tpu_custom_call" | custom-call | flops 26214400 | bytes 78337 | tf_op jit(solution)/shard_map/pack/pallas_call | solution.py:447
  9.5 0.0 all-gather.5.cloned.1.call-update
  9.6 0.0 copy-start
  9.6 10.1 %partner_part.2 = (s16[2,5136,128]{2,1,0:T(8,128)(2,1)S(1)}, bf16[512,1792]{1,0:T(8,128)(2,1)S(1)}, bf16[512,1792]{1,0:T(8,128)(2,1)S(1)}) custom-call(bf16[1024,1792]{1,0:T(8,128)(2,1)} %lam_ref.1, bf16[1792,4096]{1,0:T(8,128)(2,1)} %panel_ref.7, bf16[400,512]{1,0:T(8,128)(2,1)} %get-tuple-element.50._), custom_call_target="tpu_custom_call" | custom-call | flops 587202560 | bytes 1376257 | tf_op jit(solution)/shard_map/partner_part/pallas_call | solution.py:111
  19.7 0.0 copy-start.1
  19.7 0.1 collective-permute-start
  19.8 0.0 copy-done
  19.8 5.2 %partner_part.3._ = s16[3,2064,128]{2,1,0:T(8,128)(2,1)} custom-call(bf16[512,1792]{1,0:T(8,128)(2,1)S(1)} %get-tuple-element.53.lam_ref, bf16[1792,4096]{1,0:T(8,128)(2,1)S(1)} %copy-done, s16[2,5136,128]{2,1,0:T(8,128)(2,1)S(1)} %get-tuple-element.52._), custom_call_target="tpu_custom_call" | custom-call | flops 352321536 | bytes 917505 | tf_op jit(solution)/shard_map/partner_part/pallas_call | solution.py:143
  25.0 0.5 collective-permute-start.1
  25.5 0.0 collective-permute-done.recv_ref
  25.5 0.0 copy-done.1
  25.5 8.4 %own_x_part.1._ = s16[4,2,1296,128]{3,2,1,0:T(8,128)(2,1)} custom-call(bf16[512,1792]{1,0:T(8,128)(2,1)S(1)} %get-tuple-element.51.lam_ref, bf16[1792,4096]{1,0:T(8,128)(2,1)S(1)} %copy-done, s16[2,5136,128]{2,1,0:T(8,128)(2,1)S(1)} %collective-permute-done.recv_ref, s16[3,2064,128]{2,1,0:T(8,128)(2,1)} %partner_part.3._), custom_call_target="tpu_custom_call" | custom-call | flops 587202560 | bytes 1376257 | tf_op jit(solution)/shard_map/own_x_part/pallas_call | solution.py:238
  33.9 4.4 %all-to-all-start = ((s16[4,2,1296,128]{3,2,1,0:T(8,128)(2,1)}), s16[4,2,1296,128]{3,2,1,0:T(8,128)(2,1)S(1)}, u32[]{:S(2)}, u32[]{:S(2)}) async-start(s16[4,2,1296,128]{3,2,1,0:T(8,128)(2,1)} %own_x_part.1._), calls=%async_computation | async-start | bytes 5308416 | tf_op jit(solution)/shard_map/all_to_all | solution.py:530
  38.2 0.0 copy-start.4
  38.2 0.0 collective-permute-done.1.recv_ref
  38.2 7.6 %own_z_part.1 = (s16[3,1040,128]{2,1,0:T(8,128)(2,1)}, f32[3,4,256,128]{3,2,1,0:T(8,128)}) custom-call(bf16[512,1792]{1,0:T(8,128)(2,1)} %copy-done.1, bf16[1792,4096]{1,0:T(8,128)(2,1)} %panel_ref.7, s16[3,2064,128]{2,1,0:T(8,128)(2,1)} %collective-permute-done.1.recv_ref, s16[4,2,1296,128]{3,2,1,0:T(8,128)(2,1)} %own_x_part.1._), custom_call_target="tpu_custom_call" | custom-call | flops 352321536 | bytes 917505 | tf_op jit(solution)/shard_map/own_z_part/pallas_call | solution.py:198
  45.9 3.9 %collective-permute-start.3 = (s16[3,1040,128]{2,1,0:T(8,128)(2,1)}, s16[3,1040,128]{2,1,0:T(8,128)(2,1)S(1)}, u32[]{:S(2)}, u32[]{:S(2)}) collective-permute-start(s16[3,1040,128]{2,1,0:T(8,128)(2,1)} %get-tuple-element.55), channel_id=1, source_target_pairs={{0,2},{2,0},{1,3},{3,1},{4,6},{6,4},{5,7},{7,5},{8,10},{10,8},{9,1... | collective-permute-start | bytes 2396168 | tf_op jit(solution)/shard_map/ppermute | solution.py:526
  49.7 0.0 copy-done.4
  49.7 0.8 compare_reduce_fusion
  51.2 5.7 %all-gather.5.cloned.1.call-done = bf16[3200,512]{1,0:T(8,128)(2,1)} async-done(((bf16[400,512]{1,0:T(8,128)(2,1)}), bf16[3200,512]{1,0:T(8,128)(2,1)}) %all-gather.5.cloned.1.call-update) | async-done | bytes 3276816 | tf_op jit(solution)/shard_map/all_gather | solution.py:548
  56.9 11.0 %conditional.1 = (f32[8,2,8,2048]{3,2,1,0:T(8,128)}) conditional(s32[]{:T(128)} %convert_element_type.3, (s32[200]{0:T(256)}, s32[256]{0:T(256)S(1)}, s32[]{:T(128)}, bf16[400,2048]{1,0:T(8,128)(2,1)}, bf16[128,3200]{1,0:T(8,128)(2,1)}, /*index=5*/(), s32[]{:T(128)}, s32[]{:T(128)}, (), ()) %tuple.28, (s32[256]{0:T(256)S(1)}, s32[200]{0:T(256)}, ...), branch_computations={%region_1.2_spmd, %region_2.3_spmd} | conditional | flops 1690834048 | bytes 59298000 | solution.py:588
  56.9 0.0 copy-start.5
  56.9 0.6 copy-done.5
  57.5 10.4 %cycle_term.1 = f32[8,2,8,2048]{3,2,1,0:T(8,128)} custom-call(s32[200]{0:T(256)} %get-tuple-element.35.occ_s_ref, s32[256]{0:T(256)} %copy-done.5, s32[1,256]{1,0:T(1,128)} %bitcast.13, s32[1,2048]{1,0:T(1,128)} %get-tuple-element.37.jb_ref, bf16[128,3200]{1,0:T(8,128)(2,1)} %get-tuple-element.38.amp_ref, bf16[3200,512]{1,0:T(8,128)(2,1)} %get-tuple-element.39.packed_ref, ...), custom_call_target="tpu_custom_call" | custom-call | flops 419430400 | bytes 1843201 | tf_op jit(solution)/shard_map/cond/branch_1_fun/cycle_term/pallas_call | solution.py:504
  68.0 2.8 %all-to-all-done.recv_ref = s16[4,2,1296,128]{3,2,1,0:T(8,128)(2,1)S(1)} async-done(((s16[4,2,1296,128]{3,2,1,0:T(8,128)(2,1)}), s16[4,2,1296,128]{3,2,1,0:T(8,128)(2,1)S(1)}, u32[]{:S(2)}, u32[]{:S(2)}) %all-to-all-start) | async-done | bytes 2654240 | tf_op jit(solution)/shard_map/all_to_all | solution.py:530
  70.7 0.0 copy-start.2
  70.7 1.7 %merge_x.1 = (s16[2,656,128]{2,1,0:T(8,128)(2,1)}, f32[2,10,64,128]{3,2,1,0:T(8,128)}) custom-call(s16[4,2,1296,128]{3,2,1,0:T(8,128)(2,1)S(1)} %all-to-all-done.recv_ref, f32[8,2,8,2048]{3,2,1,0:T(8,128)} %get-tuple-element.69._.refs_3_), custom_call_target="tpu_custom_call" | custom-call | bytes 331777 | tf_op jit(solution)/shard_map/merge_x/pallas_call | solution.py:316
  72.4 0.0 copy-start.6
  72.4 0.0 copy-start.3
  72.4 1.9 %collective-permute-done.3.recv_ref = s16[3,1040,128]{2,1,0:T(8,128)(2,1)S(1)} collective-permute-done((s16[3,1040,128]{2,1,0:T(8,128)(2,1)}, s16[3,1040,128]{2,1,0:T(8,128)(2,1)S(1)}, u32[]{:S(2)}, u32[]{:S(2)}) %collective-permute-start.3) | collective-permute-done | bytes 798752 | tf_op jit(solution)/shard_map/ppermute | solution.py:526
  74.3 0.0 copy-done.2
  74.3 1.8 %merge_z.1 = s16[4,3,272,128]{3,2,1,0:T(8,128)(2,1)} custom-call(f32[3,4,256,128]{3,2,1,0:T(8,128)S(1)} %copy-done.2, s16[3,1040,128]{2,1,0:T(8,128)(2,1)S(1)} %collective-permute-done.3.recv_ref, f32[2,10,64,128]{3,2,1,0:T(8,128)} %get-tuple-element.56._.refs_0_), custom_call_target="tpu_custom_call" | custom-call | bytes 394753 | tf_op jit(solution)/shard_map/merge_z/pallas_call | solution.py:277
  76.2 4.2 %all-to-all-start.1 = ((s16[4,3,272,128]{3,2,1,0:T(8,128)(2,1)}), s16[4,3,272,128]{3,2,1,0:T(8,128)(2,1)S(1)}, u32[]{:S(2)}, u32[]{:S(2)}) async-start(s16[4,3,272,128]{3,2,1,0:T(8,128)(2,1)} %merge_z.1), calls=%async_computation.1 | async-start | bytes 1671168 | tf_op jit(solution)/shard_map/all_to_all | solution.py:530
  80.4 0.0 copy-done.6
  80.4 1.3 %collective-permute-start.2 = (s16[2,656,128]{2,1,0:T(8,128)(2,1)S(1)}, s16[2,656,128]{2,1,0:T(8,128)(2,1)S(1)}, u32[]{:S(2)}, u32[]{:S(2)}) collective-permute-start(s16[2,656,128]{2,1,0:T(8,128)(2,1)S(1)} %copy-done.6), channel_id=1, source_target_pairs={{0,2},{2,0},{1,3},{3,1},{4,6},{6,4},{5,7},{7,5},{8,10},{10,8},{9,1... | collective-permute-start | bytes 1007624 | tf_op jit(solution)/shard_map/ppermute | solution.py:526
  81.7 9.7 %collective-permute-done.2.refs_1_ = s16[2,656,128]{2,1,0:T(8,128)(2,1)S(1)} collective-permute-done((s16[2,656,128]{2,1,0:T(8,128)(2,1)S(1)}, s16[2,656,128]{2,1,0:T(8,128)(2,1)S(1)}, u32[]{:S(2)}, u32[]{:S(2)}) %collective-permute-start.2) | collective-permute-done | bytes 335904 | tf_op jit(solution)/shard_map/ppermute | solution.py:526
  91.4 2.0 %all-to-all-done.1.refs_2_ = s16[4,3,272,128]{3,2,1,0:T(8,128)(2,1)S(1)} async-done(((s16[4,3,272,128]{3,2,1,0:T(8,128)(2,1)}), s16[4,3,272,128]{3,2,1,0:T(8,128)(2,1)S(1)}, u32[]{:S(2)}, u32[]{:S(2)}) %all-to-all-start.1) | async-done | bytes 835616 | tf_op jit(solution)/shard_map/all_to_all | solution.py:530
  93.4 0.0 copy-done.3
  93.4 2.5 %finish.1 = f32[8,2,8,2048]{3,2,1,0:T(8,128)} custom-call(f32[2,10,64,128]{3,2,1,0:T(8,128)} %get-tuple-element.56._.refs_0_, s16[2,656,128]{2,1,0:T(8,128)(2,1)S(1)} %collective-permute-done.2.refs_1_, s16[4,3,272,128]{3,2,1,0:T(8,128)(2,1)S(1)} %all-to-all-done.1.refs_2_, f32[8,2,8,2048]{3,2,1,0:T(8,128)S(1)} %copy-done.3), custom_call_target="tpu_custom_call" | custom-call | bytes 524289 | tf_op jit(solution)/shard_map/finish/pallas_call | solution.py:387
Async XLA Ops:
  6.5 50.4 %all-gather.5.cloned.1.call-start = ((), (), s32[]{:S(2)}) async-start(), calls=%async_computation.3 | async-start | bytes 3686400 | tf_op jit(solution)/shard_map/all_gather | solution.py:548
  9.6 10.2 %copy-start = (bf16[1792,4096]{1,0:T(8,128)(2,1)S(1)}, bf16[1792,4096]{1,0:T(8,128)(2,1)}, u32[]{:S(2)}) copy-start(bf16[1792,4096]{1,0:T(8,128)(2,1)} %panel_ref.7) | copy-start | bytes 44040196
  19.7 5.8 %copy-start.1 = (bf16[512,1792]{1,0:T(8,128)(2,1)}, bf16[512,1792]{1,0:T(8,128)(2,1)S(1)}, u32[]{:S(2)}) copy-start(bf16[512,1792]{1,0:T(8,128)(2,1)S(1)} %get-tuple-element.51.lam_ref) | copy-start | bytes 5505028
  19.7 5.8 %collective-permute-start = (s16[2,5136,128]{2,1,0:T(8,128)(2,1)S(1)}, s16[2,5136,128]{2,1,0:T(8,128)(2,1)S(1)}, u32[]{:S(2)}, u32[]{:S(2)}) collective-permute-start(s16[2,5136,128]{2,1,0:T(8,128)(2,1)S(1)} %get-tuple-element.52._), channel_id=1, source_target_pairs={{0,1},{1,0},{2,3},{3,2},{4,5},{5,4},{6,7},{7,6},{8,9},{9,8},{10,11... | collective-permute-start | bytes 7888904 | tf_op jit(solution)/shard_map/ppermute | solution.py:526
  25.0 13.2 %collective-permute-start.1 = (s16[3,2064,128]{2,1,0:T(8,128)(2,1)}, s16[3,2064,128]{2,1,0:T(8,128)(2,1)}, u32[]{:S(2)}, u32[]{:S(2)}) collective-permute-start(s16[3,2064,128]{2,1,0:T(8,128)(2,1)} %partner_part.3._), channel_id=1, source_target_pairs={{0,1},{1,0},{2,3},{3,2},{4,5},{5,4},{6,7},{7,6},{8,9},{9,8},{10,11... | collective-permute-start | bytes 4755464 | tf_op jit(solution)/shard_map/ppermute | solution.py:526
  33.9 36.9 %all-to-all-start = ((s16[4,2,1296,128]{3,2,1,0:T(8,128)(2,1)}), s16[4,2,1296,128]{3,2,1,0:T(8,128)(2,1)S(1)}, u32[]{:S(2)}, u32[]{:S(2)}) async-start(s16[4,2,1296,128]{3,2,1,0:T(8,128)(2,1)} %own_x_part.1._), calls=%async_computation | async-start | bytes 5308416 | tf_op jit(solution)/shard_map/all_to_all | solution.py:530
  38.2 11.5 %copy-start.4 = (s32[256]{0:T(256)S(1)}, s32[256]{0:T(256)}, u32[]{:S(2)}) copy-start(s32[256]{0:T(256)} %param.13) | copy-start | bytes 3076
  45.9 28.5 %collective-permute-start.3 = (s16[3,1040,128]{2,1,0:T(8,128)(2,1)}, s16[3,1040,128]{2,1,0:T(8,128)(2,1)S(1)}, u32[]{:S(2)}, u32[]{:S(2)}) collective-permute-start(s16[3,1040,128]{2,1,0:T(8,128)(2,1)} %get-tuple-element.55), channel_id=1, source_target_pairs={{0,2},{2,0},{1,3},{3,1},{4,6},{6,4},{5,7},{7,5},{8,10},{10,8},{9,1... | collective-permute-start | bytes 2396168 | tf_op jit(solution)/shard_map/ppermute | solution.py:526
  56.9 0.6 copy-start.5
  70.7 3.6 %copy-start.2 = (f32[3,4,256,128]{3,2,1,0:T(8,128)S(1)}, f32[3,4,256,128]{3,2,1,0:T(8,128)}, u32[]{:S(2)}) copy-start(f32[3,4,256,128]{3,2,1,0:T(8,128)} %get-tuple-element.58.keep_ref) | copy-start | bytes 4718596
  72.4 8.0 %copy-start.6 = (s16[2,656,128]{2,1,0:T(8,128)(2,1)S(1)}, s16[2,656,128]{2,1,0:T(8,128)(2,1)}, u32[]{:S(2)}) copy-start(s16[2,656,128]{2,1,0:T(8,128)(2,1)} %get-tuple-element.57) | copy-start | bytes 1007620
  72.4 21.0 %copy-start.3 = (f32[8,2,8,2048]{3,2,1,0:T(8,128)S(1)}, f32[8,2,8,2048]{3,2,1,0:T(8,128)}, u32[]{:S(2)}) copy-start(f32[8,2,8,2048]{3,2,1,0:T(8,128)} %get-tuple-element.69._.refs_3_) | copy-start | bytes 3145732
  76.2 17.2 %all-to-all-start.1 = ((s16[4,3,272,128]{3,2,1,0:T(8,128)(2,1)}), s16[4,3,272,128]{3,2,1,0:T(8,128)(2,1)S(1)}, u32[]{:S(2)}, u32[]{:S(2)}) async-start(s16[4,3,272,128]{3,2,1,0:T(8,128)(2,1)} %merge_z.1), calls=%async_computation.1 | async-start | bytes 1671168 | tf_op jit(solution)/shard_map/all_to_all | solution.py:530
  80.4 11.0 %collective-permute-start.2 = (s16[2,656,128]{2,1,0:T(8,128)(2,1)S(1)}, s16[2,656,128]{2,1,0:T(8,128)(2,1)S(1)}, u32[]{:S(2)}, u32[]{:S(2)}) collective-permute-start(s16[2,656,128]{2,1,0:T(8,128)(2,1)S(1)} %copy-done.6), channel_id=1, source_target_pairs={{0,2},{2,0},{1,3},{3,1},{4,6},{6,4},{5,7},{7,5},{8,10},{10,8},{9,1... | collective-permute-start | bytes 1007624 | tf_op jit(solution)/shard_map/ppermute | solution.py:526
Sparse Core Ops, SparseCore 0:
  9.7 47.1 all-gather.4
